TPU v7x, 256 devices: a whole 4x4x8 slice. The times are simulated.
256 devices in a mesh: dp: 2 (over y_hi), row: 32 (over y_lo, z, core), chan: 4 (over x).
Axes of the slice: x: 4, y: 4 (y_hi: 2, y_lo: 2; y = y_hi * 2 + y_lo), z: 8, core: 2. Of those that a mesh axis runs over, the one named last changes fastest.
Arguments:
- pair_rep: bfloat16 [2048, 1024, 128], P(('dp', 'row', 'chan')), parts along dimension 0, may hold values from -16 to 16
- token_mask: int32 [2048], P('dp'), parts along dimension 0, may hold values from 0 to 1, as said below
- w_a_gate: bfloat16 [128, 128], replicated, may hold values from -0.5 to 0.5
- w_a_proj: bfloat16 [128, 128], replicated, may hold values from -0.5 to 0.5
- w_b_gate: bfloat16 [128, 128], replicated, may hold values from -0.5 to 0.5
- w_b_proj: bfloat16 [128, 128], replicated, may hold values from -0.5 to 0.5
- w_gate: bfloat16 [128, 128], replicated, may hold values from -0.5 to 0.5
- w_out: bfloat16 [128, 128], replicated, may hold values from -0.5 to 0.5
- w_dist: bfloat16 [128, 64], replicated, may hold values from -0.5 to 0.5
Outputs:
- updated_pair: bfloat16 [2048, 1024, 128], P(('dp', 'row', 'chan')), parts along dimension 0
- dist_logits: float32 [64, 2048, 1024], P(None, ('dp', 'row', 'chan')), parts along dimension 1
There are 2 independent parts, one for each index of `dp`. A program takes and returns all parts, laid end to end along the dimension named above; an argument that names none is the same for every part. Nothing has to cross between parts.
Inputs may be any that keep to these rules, and one draw needn't show every extreme that they name: `token_mask`: the first token is 1 and the last is 0; tokens between may be 0.
All inputs are finite; a program needn't handle non-finite values.
Results may differ from a plain program's by a relative error of at most 0.0049.
Values may be sent and summed in bfloat16 or wider, within the bound.
No kernel may reach another device: no remote copies, remote signals or barrier semaphores. Data moves between devices by JAX's collectives and lax.ppermute only.
A program may use at most 128 MiB of HBM per device.

v0:
```python
import jax
import jax.numpy as jnp
from jax import lax
from jax.sharding import PartitionSpec as P

epsilon = 1e-05


def layer_norm(values, axis_index):
    values = values.astype(jnp.float32)
    center = values - jnp.mean(values, axis=axis_index, keepdims=True)
    second = jnp.mean(center * center, axis=axis_index, keepdims=True)
    return center * lax.rsqrt(second + epsilon)


def gated_side(normed, w_first, w_second, pair_keep):
    gate_part = jnp.einsum("kic,ch->hki", normed, w_first, preferred_element_type=jnp.float32)
    proj_part = jnp.einsum("kic,ch->hki", normed, w_second, preferred_element_type=jnp.float32)
    return (jax.nn.sigmoid(gate_part) * proj_part * pair_keep[None]).astype(jnp.bfloat16)


def finish(out_rows, normed, base_rows, w_gate, w_out):
    gate_vals = jax.nn.sigmoid(
        jnp.einsum("ijc,cd->ijd", normed, w_gate, preferred_element_type=jnp.float32)
    )
    normal_out = layer_norm(out_rows, 0).astype(jnp.bfloat16)
    projected = jnp.einsum("hij,hc->ijc", normal_out, w_out, preferred_element_type=jnp.float32)
    return (base_rows.astype(jnp.float32) + gate_vals * projected).astype(jnp.bfloat16)


def mirror_split(grid, devices):
    height, length, depth = grid.shape
    blocks = grid.reshape(height, devices, height, depth)
    return jnp.swapaxes(blocks, 0, 2)


def to_row_layout(stacked):
    arrived = lax.all_to_all(stacked, ("row", "chan"), split_axis=2, concat_axis=1, tiled=True)
    return arrived


def local(pair_rep, token_mask, w_a_gate, w_a_proj, w_b_gate, w_b_proj, w_gate, w_out, w_dist):
    rows_here, columns, channels = pair_rep.shape
    devices = lax.axis_size(("row", "chan"))
    offset = lax.axis_index(("row", "chan")) * rows_here
    present = token_mask.astype(jnp.float32)
    own_present = lax.dynamic_slice_in_dim(present, offset, rows_here)
    pair_keep = own_present[:, None] * present[None, :]
    normed = layer_norm(pair_rep, 2).astype(jnp.bfloat16)
    both_sides = jnp.stack(
        [
            gated_side(normed, w_a_gate, w_a_proj, pair_keep),
            gated_side(normed, w_b_gate, w_b_proj, pair_keep),
        ]
    )
    by_channel = lax.all_to_all(
        both_sides, ("row", "chan"), split_axis=1, concat_axis=2, tiled=True
    )
    product = jnp.einsum(
        "hki,hkj->hij", by_channel[0], by_channel[1], preferred_element_type=jnp.float32
    ).astype(jnp.bfloat16)
    returned = to_row_layout(product[None])
    updated = finish(returned[0], normed, pair_rep, w_gate, w_out)
    updated_mirror = lax.all_to_all(
        mirror_split(updated, devices), ("row", "chan"), split_axis=1, concat_axis=1, tiled=True
    ).reshape(rows_here, columns, channels)
    logits = jnp.einsum("ijc,cb->bij", updated, w_dist, preferred_element_type=jnp.float32)
    logits = logits + jnp.einsum(
        "ijc,cb->bij", updated_mirror, w_dist, preferred_element_type=jnp.float32
    )
    return (updated, logits)


def solution(mesh):
    in_specs = (P(("dp", "row", "chan"), None, None), P("dp"), P(), P(), P(), P(), P(), P(), P())
    out_specs = (P(("dp", "row", "chan"), None, None), P(None, ("dp", "row", "chan"), None))
    return jax.shard_map(local, mesh=mesh, in_specs=in_specs, out_specs=out_specs, check_vma=False)
```

profile of v0, /device:TPU:1, one launch (start us, length us, event | category | flops | bytes accessed | tf_op | source)
XLA Modules:
  0.0 347.6 jit_solution(4379113230889695735)
XLA Ops:
  3.7 3.6 %fusion.2 = f32[8,1024]{1,0:T(8,128)S(1)} fusion(bf16[8,1024,128]{2,1,0:T(8,128)(2,1)} %param.9, f32[8,1024]{1,0:T(8,128)S(1)} %broadcast_multiply_fusion.2), kind=kLoop, calls=%fused_computation.5 | loop fusion | flops 4186112 | bytes 2162688 | tf_op jit(solution)/shard_map/reduce_sum | solution.py:12
  7.5 3.7 %fusion.23 = f32[8,1024,128]{2,1,0:T(8,128)S(1)} fusion(bf16[128,128]{1,0:T(8,128)(2,1)S(1)} %copy-done, bf16[8,1024,128]{2,1,0:T(8,128)(2,1)S(1)} %copy-done.2, f32[8,1024]{1,0:T(8,128)S(1)} %get-tuple-element.8, f32[8,1024]{1,0:T(8,128)S(1)} %broadcast_multiply_fusion.2), kind=kOutput, calls=%fused_computation.32 | convolution fusion | flops 272629760 | bytes 6389760 | tf_op jit(solution)/shard_map/kic,ch->hki/dot_general | solution.py:17
  11.2 3.7 %fusion.20 = f32[8,1024,128]{2,1,0:T(8,128)S(1)} fusion(bf16[128,128]{1,0:T(8,128)(2,1)S(1)} %copy-done.6, bf16[8,1024,128]{2,1,0:T(8,128)(2,1)S(1)} %copy-done.2, f32[8,1024]{1,0:T(8,128)S(1)} %get-tuple-element.8, f32[8,1024]{1,0:T(8,128)S(1)} %broadcast_multiply_fusion.2), kind=kOutput, calls=%fused_computation.29 | convolution fusion | flops 272629760 | bytes 6389760 | tf_op jit(solution)/shard_map/kic,ch->hki/dot_general | solution.py:17
  14.9 3.9 %fusion.13 = bf16[1,128,8,1024]{1,3,2,0:T(8,128)(2,1)S(1)} fusion(f32[8,1024]{1,0:T(8,128)S(1)} %get-tuple-element.9, f32[8,1024,128]{2,1,0:T(8,128)S(1)} %fusion.23, bf16[128,128]{1,0:T(8,128)(2,1)S(1)} %copy-done.8, bf16[8,1024,128]{2,1,0:T(8,128)(2,1)S(1)} %copy-done.2, f32[8,1024]{1,0:T(8,128)S(1)} %get-tuple-element.8, ...), kind=kOutput, calls=%fused_computation.24 | convolution fusion | flops 278921216 | bytes 8519680 | tf_op jit(solution)/shard_map/kic,ch->hki/dot_general | solution.py:18
  18.8 3.9 %fusion.14 = bf16[1,128,8,1024]{1,3,2,0:T(8,128)(2,1)S(1)} fusion(f32[8,1024]{1,0:T(8,128)S(1)} %get-tuple-element.9, f32[8,1024,128]{2,1,0:T(8,128)S(1)} %fusion.20, bf16[128,128]{1,0:T(8,128)(2,1)S(1)} %copy-done.9, bf16[8,1024,128]{2,1,0:T(8,128)(2,1)S(1)} %copy-done.2, f32[8,1024]{1,0:T(8,128)S(1)} %get-tuple-element.8, ...), kind=kOutput, calls=%fused_computation.25 | convolution fusion | flops 278921216 | bytes 8519680 | tf_op jit(solution)/shard_map/kic,ch->hki/dot_general | solution.py:18
  25.0 6.8 %copy.15 = bf16[2,128,8,1024]{3,2,0,1:T(8,128)(2,1)} copy(bf16[2,128,8,1024]{1,3,2,0:T(8,128)(2,1)} %pad_maximum_fusion) | data formatting | bytes 8388608 | tf_op jit(solution)/shard_map/stack | solution.py:50
  31.9 110.5 %all_to_all.23 = bf16[2,128,8,1024]{3,2,0,1:T(8,128)(2,1)S(1)} all-to-all(bf16[2,128,8,1024]{3,2,0,1:T(8,128)(2,1)} %copy.15), channel_id=1, replica_groups=mesh['dp'=2,'row'=32,'chan'=4] {'row','chan'}, dimensions={1} | all-to-all | bytes 8388608 | tf_op jit(solution)/shard_map/all_to_all | solution.py:56
  144.9 4.2 %copy.24 = bf16[1,128,8,1024]{1,3,2,0:T(8,128)(2,1)} copy(bf16[1,128,8,1024]{3,2,0,1:T(8,128)(2,1)} %get-tuple-element.6) | data formatting | bytes 4194304
  149.0 5.1 %fusion.15 = bf16[1,1,1024,1024]{3,2,1,0:T(8,128)(2,1)S(1)} fusion(bf16[1,128,8,1024]{3,2,0,1:T(8,128)(2,1)} %get-tuple-element.7, bf16[1,128,8,1024]{1,3,2,0:T(8,128)(2,1)} %copy.24), kind=kOutput, calls=%fused_computation.26 | convolution fusion | flops 2148532224 | bytes 6291456 | tf_op jit(solution)/shard_map/hki,hkj->hij/dot_general | solution.py:59
  154.1 5.2 %copy.42 = bf16[1,1,1024,1024]{3,1,0,2:T(2,128)(2,1)} copy(bf16[1,1,1024,1024]{3,2,1,0:T(8,128)(2,1)S(1)} %fusion.15) | data formatting | bytes 4194304 | tf_op jit(solution)/shard_map/broadcast_in_dim | solution.py:62
  159.8 14.1 %reduce = bf16[1024,1024]{1,0:T(8,128)(2,1)} reduce(bf16[1024,1,1,1024]{3,2,1,0:T(2,128)(2,1)} %bitcast.70, bf16[]{:T(256)} %broadcast.94), dimensions={1,2}, to_apply=%bitcast.69.reduce_sub_computation | reduce | bytes 4194306
  173.9 4.4 %reshape.105 = bf16[128,2,4096]{2,1,0:T(2,128)(2,1)} reshape(bf16[1024,1024]{1,0:T(8,128)(2,1)} %reduce) | data formatting | bytes 4194304
  178.3 9.6 %all-to-all-start.1 = ((bf16[128,2,4096]{2,1,0:T(2,128)(2,1)}), bf16[128,2,4096]{2,1,0:T(2,128)(2,1)}, u32[]{:S(2)}, u32[]{:S(2)}) async-start(bf16[128,2,4096]{2,1,0:T(2,128)(2,1)} %reshape.105), calls=%async_computation.1 | async-start | bytes 4194304 | tf_op jit(solution)/shard_map/all_to_all | solution.py:38
  187.9 5.2 %fusion.25 = f32[8,1024,128]{2,1,0:T(8,128)} fusion(bf16[128,128]{1,0:T(8,128)(2,1)S(1)} %copy-done.7, bf16[8,1024,128]{2,1,0:T(8,128)(2,1)S(1)} %copy-done.2, f32[8,1024]{1,0:T(8,128)S(1)} %get-tuple-element.8, f32[8,1024]{1,0:T(8,128)S(1)} %broadcast_multiply_fusion.2), kind=kOutput, calls=%fused_computation.34 | convolution fusion | flops 272629760 | bytes 6389760 | tf_op jit(solution)/shard_map/ijc,cd->ijd/dot_general | solution.py:24
  193.1 46.7 %all-to-all-done.1 = bf16[128,2,4096]{2,1,0:T(2,128)(2,1)} async-done(((bf16[128,2,4096]{2,1,0:T(2,128)(2,1)}), bf16[128,2,4096]{2,1,0:T(2,128)(2,1)}, u32[]{:S(2)}, u32[]{:S(2)}) %all-to-all-start.1) | async-done | bytes 2097184 | tf_op jit(solution)/shard_map/all_to_all | solution.py:38
  239.8 13.8 %reshape.106 = bf16[1024,1,1,1024]{3,2,1,0:T(2,128)(2,1)} reshape(bf16[128,2,4096]{2,1,0:T(2,128)(2,1)} %all-to-all-done.1) | data formatting | bytes 4194304
  253.6 6.5 %bitcast_convert_fusion.1 = f32[1,1,1024,1024]{3,1,0,2:T(1,128)S(1)} fusion(bf16[1024,1,1,1024]{3,2,1,0:T(2,128)(2,1)} %reshape.106), kind=kLoop, calls=%fused_computation.46 | loop fusion | flops 1048576 | bytes 6291456 | tf_op jit(solution)/shard_map/convert_element_type | solution.py:10
  260.7 3.0 copy.41
  263.7 5.4 %copy.19 = f32[128,8,1024]{0,2,1:T(8,128)} copy(f32[128,8,1024]{2,1,0:T(8,128)} %bitcast.71) | data formatting | bytes 8388608 | tf_op jit(solution)/shard_map/convert_element_type | solution.py:10
  269.1 4.1 %multiply_reduce_fusion = f32[8,1024]{1,0:T(8,128)S(1)} fusion(f32[128,8,1024]{0,2,1:T(8,128)} %copy.19, f32[8,1024]{1,0:T(8,128)S(1)} %broadcast_multiply_fusion.1), kind=kLoop, calls=%fused_computation.14 | loop fusion | flops 3137536 | bytes 4259840 | tf_op jit(solution)/shard_map/reduce_sum | solution.py:12
  273.3 6.1 %fusion.4 = bf16[8,1024,128]{2,1,0:T(8,128)(2,1)S(1)} fusion(bf16[8,1024,128]{2,1,0:T(8,128)(2,1)S(1)} %copy-done.2, f32[8,1024,128]{2,1,0:T(8,128)} %fusion.25, f32[128,8,1024]{0,2,1:T(8,128)S(1)} %copy-done.3, f32[8,1024]{1,0:T(8,128)S(1)} %add_rsqrt_fusion, f32[8,1024]{1,0:T(8,128)S(1)} %broadcast_multiply_fusion.1, bf16[128,128]{1,0:T(8,128)(2,1)S(1)} %copy-done.10), kind=kOutput, calls=%fused_computation.7 | convolution fusion | flops 278921216 | bytes 12681216 | tf_op jit(solution)/shard_map/hij,hc->ijc/dot_general | solution.py:27
  282.6 7.7 %all-to-all-start.2 = ((bf16[8,128,8,128]{3,0,2,1:T(8,128)(2,1)}), bf16[8,128,8,128]{3,0,2,1:T(8,128)(2,1)S(1)}, u32[]{:S(2)}, u32[]{:S(2)}) async-start(bf16[8,128,8,128]{3,0,2,1:T(8,128)(2,1)} %copy_bitcast_fusion.3), calls=%async_computation.2 | async-start | bytes 4194304 | tf_op jit(solution)/shard_map/all_to_all | solution.py:64
  290.3 3.8 %fusion.28 = f32[8,1024,64]{1,2,0:T(8,128)} fusion(bf16[8,1024,128]{2,1,0:T(8,128)(2,1)} %copy-done.4, bf16[128,64]{0,1:T(8,128)(2,1)S(1)} %copy-done.5), kind=kOutput, calls=%fused_computation.39 | convolution fusion | flops 134217728 | bytes 4210688 | tf_op jit(solution)/shard_map/ijc,cb->bij/dot_general | solution.py:67
  294.1 48.4 %all-to-all-done.2 = bf16[8,128,8,128]{3,0,2,1:T(8,128)(2,1)S(1)} async-done(((bf16[8,128,8,128]{3,0,2,1:T(8,128)(2,1)}), bf16[8,128,8,128]{3,0,2,1:T(8,128)(2,1)S(1)}, u32[]{:S(2)}, u32[]{:S(2)}) %all-to-all-start.2) | async-done | bytes 2097184 | tf_op jit(solution)/shard_map/all_to_all | solution.py:64
  (36 shorter events, 17.4 us)
Async XLA Ops:
  0.6 6.9 %copy-start = (bf16[128,128]{1,0:T(8,128)(2,1)S(1)}, bf16[128,128]{1,0:T(8,128)(2,1)}, u32[]{:S(2)}) copy-start(bf16[128,128]{1,0:T(8,128)(2,1)} %param.11) | copy-start | bytes 98308
  0.6 6.9 %copy-start.2 = (bf16[8,1024,128]{2,1,0:T(8,128)(2,1)S(1)}, bf16[8,1024,128]{2,1,0:T(8,128)(2,1)}, u32[]{:S(2)}) copy-start(bf16[8,1024,128]{2,1,0:T(8,128)(2,1)} %param.9) | copy-start | bytes 6291460
  3.7 7.4 %copy-start.6 = (bf16[128,128]{1,0:T(8,128)(2,1)S(1)}, bf16[128,128]{1,0:T(8,128)(2,1)}, u32[]{:S(2)}) copy-start(bf16[128,128]{1,0:T(8,128)(2,1)} %param.13) | copy-start | bytes 98308
  11.2 3.7 %copy-start.8 = (bf16[128,128]{1,0:T(8,128)(2,1)S(1)}, bf16[128,128]{1,0:T(8,128)(2,1)}, u32[]{:S(2)}) copy-start(bf16[128,128]{1,0:T(8,128)(2,1)} %param.12) | copy-start | bytes 98308
  14.9 3.9 %copy-start.9 = (bf16[128,128]{1,0:T(8,128)(2,1)S(1)}, bf16[128,128]{1,0:T(8,128)(2,1)}, u32[]{:S(2)}) copy-start(bf16[128,128]{1,0:T(8,128)(2,1)} %param.14) | copy-start | bytes 98308
  173.9 14.0 %copy-start.7 = (bf16[128,128]{1,0:T(8,128)(2,1)S(1)}, bf16[128,128]{1,0:T(8,128)(2,1)}, u32[]{:S(2)}) copy-start(bf16[128,128]{1,0:T(8,128)(2,1)} %param.15) | copy-start | bytes 98308
  178.3 61.5 %all-to-all-start.1 = ((bf16[128,2,4096]{2,1,0:T(2,128)(2,1)}), bf16[128,2,4096]{2,1,0:T(2,128)(2,1)}, u32[]{:S(2)}, u32[]{:S(2)}) async-start(bf16[128,2,4096]{2,1,0:T(2,128)(2,1)} %reshape.105), calls=%async_computation.1 | async-start | bytes 4194304 | tf_op jit(solution)/shard_map/all_to_all | solution.py:38
  269.1 4.1 %copy-start.3 = (f32[128,8,1024]{0,2,1:T(8,128)S(1)}, f32[128,8,1024]{0,2,1:T(8,128)}, u32[]{:S(2)}) copy-start(f32[128,8,1024]{0,2,1:T(8,128)} %copy.19) | copy-start | bytes 12582916
  269.1 4.1 %copy-start.10 = (bf16[128,128]{1,0:T(8,128)(2,1)S(1)}, bf16[128,128]{1,0:T(8,128)(2,1)}, u32[]{:S(2)}) copy-start(bf16[128,128]{1,0:T(8,128)(2,1)} %param.16) | copy-start | bytes 98308
  279.4 1.3 copy-start.4
  280.7 9.6 %copy-start.5 = (bf16[128,64]{0,1:T(8,128)(2,1)S(1)}, bf16[128,64]{0,1:T(8,128)(2,1)}, u32[]{:S(2)}) copy-start(bf16[128,64]{0,1:T(8,128)(2,1)} %param.17) | copy-start | bytes 49156
  282.6 59.9 %all-to-all-start.2 = ((bf16[8,128,8,128]{3,0,2,1:T(8,128)(2,1)}), bf16[8,128,8,128]{3,0,2,1:T(8,128)(2,1)S(1)}, u32[]{:S(2)}, u32[]{:S(2)}) async-start(bf16[8,128,8,128]{3,0,2,1:T(8,128)(2,1)} %copy_bitcast_fusion.3), calls=%async_computation.2 | async-start | bytes 4194304 | tf_op jit(solution)/shard_map/all_to_all | solution.py:64
  290.3 57.3 %copy-start.1 = (bf16[128,128]{1,0:T(8,128)(2,1)S(1)}, bf16[128,128]{1,0:T(8,128)(2,1)}, u32[]{:S(2)}) copy-start(bf16[128,128]{1,0:T(8,128)(2,1)} %param.11) | copy-start | bytes 98308
where the time goes:
time: 350 us; the launch traced here: 348 us
  blocking collectives  111 us (32%)
  waiting for transfers between devices  95.1 us (27%)
  local copies, waits for them, and re-layouts  51.6 us (15%)
  matrix products  37.8 us (11%)
  other arithmetic  34.3 us (10%)
  starting transfers between devices  17.3 us (5%)
    all_to_all x1, blocking collectives, local(): lax.all_to_all(both_sides, ('row', 'chan'), split_axis=1, concat_axis=2,...  111 us
    all_to_all x1, waiting for transfers between devices, local(): lax.all_to_all(mirror_split(updated, devices), ('row', 'chan'), split_axi...  48.4 us
    all_to_all x1, waiting for transfers between devices, to_row_layout(): lax.all_to_all(stacked, ('row', 'chan'), split_axis=2, concat_axis=1, til...  46.7 us
    unnamed x28, local copies, waits for them, and re-layouts  29.8 us
    unnamed x1, other arithmetic  14.1 us
    all_to_all x1, starting transfers between devices, to_row_layout(): lax.all_to_all(stacked, ('row', 'chan'), split_axis=2, concat_axis=1, til...  9.63 us
    dot_general x2, matrix products, gated_side(): jnp.einsum('kic,ch->hki', normed, w_second, preferred_element_type=jnp.fl...  7.82 us
    reduce_sum x2, other arithmetic, layer_norm(): second = jnp.mean(center * center, axis=axis_index, keepdims=True)  7.69 us
  transfers between devices with their start and end apart: 2, of which 2 were waited for; matrix products, arithmetic and copies ran while one was open for 3% of the time, Pallas kernels for 0%

commit v1 on v0

v1 whole, which is shorter than its diff:
```python
import jax
import jax.numpy as jnp
from jax import lax
from jax.experimental import pallas as pl
from jax.experimental.pallas import tpu as pltpu
from jax.sharding import PartitionSpec as P

EPS = 1e-05
GROUP = ("row", "chan")
ROWS = 8
LANES = 128
VMEM_LIMIT = 48 * 1024 * 1024

F32 = jnp.float32
BF16 = jnp.bfloat16


def params():
    return pltpu.CompilerParams(vmem_limit_bytes=VMEM_LIMIT)


def sides_kernel(own_ref, mask_ref, x_ref, wag_ref, wap_ref, wbg_ref, wbp_ref, normed_ref, sides_ref, scratch):
    rows, wide, channels = x_ref.shape
    x = x_ref[...].astype(F32).reshape(rows * wide, channels)
    center = x - jnp.mean(x, axis=1, keepdims=True)
    second = jnp.mean(center * center, axis=1, keepdims=True)
    normed = (center * lax.rsqrt(second + EPS)).astype(BF16)
    normed_ref[...] = normed.reshape(x_ref.shape)
    mask = mask_ref[0].astype(F32)
    for side, (gate_ref, proj_ref) in enumerate(((wag_ref, wap_ref), (wbg_ref, wbp_ref))):
        gate = lax.dot_general(gate_ref[...], normed, (((0,), (1,)), ((), ())), preferred_element_type=F32)
        proj = lax.dot_general(proj_ref[...], normed, (((0,), (1,)), ((), ())), preferred_element_type=F32)
        both = jax.nn.sigmoid(gate) * proj
        for k in range(rows):
            keep = mask * own_ref[k].astype(F32)
            scratch[pl.ds(k, LANES, stride=rows), :] = both[:, k * wide : (k + 1) * wide] * keep
        sides_ref[:, side] = scratch[...].reshape(LANES, rows, wide).astype(BF16)


def make_sides(pair_rep, own_mask, token_mask, w_a_gate, w_a_proj, w_b_gate, w_b_proj):
    rows, columns, channels = pair_rep.shape
    steps = columns // LANES
    weight = pl.BlockSpec((channels, LANES), lambda g: (0, 0))
    return pl.pallas_call(
        sides_kernel,
        grid=(steps,),
        in_specs=[
            pl.BlockSpec(memory_space=pltpu.SMEM),
            pl.BlockSpec((1, 1, LANES), lambda g: (g, 0, 0)),
            pl.BlockSpec((rows, LANES, channels), lambda g: (0, g, 0)),
            weight,
            weight,
            weight,
            weight,
        ],
        out_specs=[
            pl.BlockSpec((rows, LANES, channels), lambda g: (0, g, 0)),
            pl.BlockSpec((LANES, 2, rows, LANES), lambda g: (0, 0, 0, g)),
        ],
        out_shape=[
            jax.ShapeDtypeStruct(pair_rep.shape, BF16),
            jax.ShapeDtypeStruct((LANES, 2, rows, columns), BF16),
        ],
        scratch_shapes=[pltpu.VMEM((rows * LANES, LANES), F32)],
        compiler_params=params(),
        name="sides",
    )(own_mask, token_mask.reshape(steps, 1, LANES), pair_rep, w_a_gate, w_a_proj, w_b_gate, w_b_proj)


def product_kernel(left_ref, right_ref, out_ref):
    depth = right_ref.shape[0] * right_ref.shape[2]
    left = left_ref[:, 0].reshape(depth, left_ref.shape[3])
    right = right_ref[:, 0].reshape(depth, right_ref.shape[3])
    prod = lax.dot_general(left, right, (((0,), (0,)), ((), ())), preferred_element_type=F32)
    out_ref[...] = prod.reshape(out_ref.shape).astype(BF16)


def make_product(sides):
    sources, _, rows, columns = sides.shape
    block = 256
    return pl.pallas_call(
        product_kernel,
        grid=(columns // block,),
        in_specs=[
            pl.BlockSpec((sources, 1, rows, block), lambda g: (0, 0, 0, g)),
            pl.BlockSpec((sources, 1, rows, columns), lambda g: (0, 1, 0, 0)),
        ],
        out_specs=pl.BlockSpec((block // rows, rows, columns), lambda g: (g, 0, 0)),
        out_shape=jax.ShapeDtypeStruct((columns // rows, rows, columns), BF16),
        compiler_params=params(),
        name="product",
    )(sides, sides)


def finish_kernel(
    x_ref, base_ref, normed_ref, wg_ref, wo_ref, wd_ref, w8_ref, upd_ref, own_ref, mirror_ref, scratch, wide_ref, stage
):
    rows, wide, channels = base_ref.shape
    owners = wide // rows
    bins = wd_ref.shape[1]
    x = x_ref[...].astype(F32)
    center = x - jnp.mean(x, axis=0, keepdims=True)
    second = jnp.mean(center * center, axis=0, keepdims=True)
    scratch[...] = (center * lax.rsqrt(second + EPS)).reshape(scratch.shape)
    tri = jnp.concatenate(
        [scratch[pl.ds(r, LANES, stride=rows), :].astype(BF16) for r in range(rows)], axis=1
    )
    projected = lax.dot_general(tri, wo_ref[...], (((0,), (0,)), ((), ())), preferred_element_type=F32)
    normed = normed_ref[...].reshape(rows * wide, channels)
    gate = jax.nn.sigmoid(jnp.dot(normed, wg_ref[...], preferred_element_type=F32))
    base = base_ref[...].reshape(rows * wide, channels).astype(F32)
    updated = (base + gate * projected).astype(BF16)
    upd_ref[...] = updated.reshape(upd_ref.shape)
    wide_ref[...] = updated.astype(F32)
    own = lax.dot_general(wd_ref[...], updated, (((0,), (1,)), ((), ())), preferred_element_type=F32)
    for r in range(rows):
        stage[pl.ds(r, bins, stride=rows), :] = own[:, r * wide : (r + 1) * wide]
    own_ref[...] = stage[...].reshape(own_ref.shape)
    picks = []
    for s in range(rows):
        parts = [wide_ref[pl.ds(d * rows + s, rows, stride=wide), :] for d in range(owners)]
        picks.append(jnp.concatenate(parts, axis=0).astype(BF16))
    mirror = jnp.dot(jnp.concatenate(picks, axis=1), w8_ref[...], preferred_element_type=F32)
    mirror_ref[...] = mirror.reshape(mirror_ref.shape).astype(BF16)


def make_finish(product, pair_rep, normed, w_gate, w_out, w_dist, w8):
    rows, columns, channels = pair_rep.shape
    bins = w_dist.shape[1]
    block = lambda g: (0, g, 0)
    fixed = lambda g: (0, 0)
    owners = LANES // rows
    return pl.pallas_call(
        finish_kernel,
        grid=(columns // LANES,),
        in_specs=[
            pl.BlockSpec((LANES, rows, LANES), lambda g: (0, 0, g)),
            pl.BlockSpec((rows, LANES, channels), block),
            pl.BlockSpec((rows, LANES, channels), block),
            pl.BlockSpec(w_gate.shape, fixed),
            pl.BlockSpec(w_out.shape, fixed),
            pl.BlockSpec(w_dist.shape, fixed),
            pl.BlockSpec(w8.shape, fixed),
        ],
        out_specs=[
            pl.BlockSpec((rows, LANES, channels), block),
            pl.BlockSpec((bins, rows, LANES), lambda g: (0, 0, g)),
            pl.BlockSpec((owners, rows, bins * rows), lambda g: (g, 0, 0)),
        ],
        out_shape=[
            jax.ShapeDtypeStruct(pair_rep.shape, BF16),
            jax.ShapeDtypeStruct((bins, rows, columns), F32),
            jax.ShapeDtypeStruct((columns // rows, rows, bins * rows), BF16),
        ],
        scratch_shapes=[
            pltpu.VMEM((LANES * rows, LANES), F32),
            pltpu.VMEM((rows * LANES, channels), F32),
            pltpu.VMEM((bins * rows, LANES), F32),
        ],
        compiler_params=params(),
        name="finish",
    )(product, pair_rep, normed, w_gate, w_out, w_dist, w8)


def add_kernel(own_ref, mirror_ref, out_ref):
    deep, rows, columns = own_ref.shape
    mirror = mirror_ref[...].reshape(columns, deep * rows)
    out_ref[...] = own_ref[...] + mirror.astype(F32).T.reshape(deep, rows, columns)


def make_add(own, mirror):
    bins, rows, columns = own.shape
    deep = LANES // rows
    return pl.pallas_call(
        add_kernel,
        grid=(bins // deep,),
        in_specs=[
            pl.BlockSpec((deep, rows, columns), lambda g: (g, 0, 0)),
            pl.BlockSpec((columns // rows, rows, LANES), lambda g: (0, 0, g)),
        ],
        out_specs=pl.BlockSpec((deep, rows, columns), lambda g: (g, 0, 0)),
        out_shape=jax.ShapeDtypeStruct(own.shape, F32),
        compiler_params=params(),
        name="add",
    )(own, mirror)


def exchange(values):
    return lax.all_to_all(values, GROUP, split_axis=0, concat_axis=0, tiled=True)


def spread_bins(w_dist):
    channels, bins = w_dist.shape
    repeated = jnp.repeat(w_dist, ROWS, axis=1)
    which = jnp.arange(bins * ROWS) % ROWS
    chosen = which[None, None, :] == jnp.arange(ROWS)[:, None, None]
    return jnp.where(chosen, repeated[None], jnp.zeros((), BF16)).reshape(ROWS * channels, bins * ROWS)


def local(pair_rep, token_mask, w_a_gate, w_a_proj, w_b_gate, w_b_proj, w_gate, w_out, w_dist):
    rows = pair_rep.shape[0]
    own_mask = lax.dynamic_slice_in_dim(token_mask, lax.axis_index(GROUP) * rows, rows)
    normed, sides = make_sides(pair_rep, own_mask, token_mask, w_a_gate, w_a_proj, w_b_gate, w_b_proj)
    sides = exchange(sides)
    product = exchange(make_product(sides))
    updated, own, mirror = make_finish(
        product, pair_rep, normed, w_gate, w_out, w_dist, spread_bins(w_dist)
    )
    logits = make_add(own, exchange(mirror))
    return (updated, logits)


def solution(mesh):
    in_specs = (P(("dp", "row", "chan"), None, None), P("dp"), P(), P(), P(), P(), P(), P(), P())
    out_specs = (P(("dp", "row", "chan"), None, None), P(None, ("dp", "row", "chan"), None))
    return jax.shard_map(local, mesh=mesh, in_specs=in_specs, out_specs=out_specs, check_vma=False)
```

time: 350 us -> 247 us (0.71)
  local copies, waits for them, and re-layouts: 51.6 us -> 7.66 us
  waiting for transfers between devices: 95.1 us -> 51.8 us
  matrix products: 37.8 us -> 0 us
  blocking collectives: 111 us -> 148 us
  other arithmetic: 34.3 us -> 0.09 us
  Pallas kernels: 0 us -> 28.9 us
  starting transfers between devices: 17.3 us -> 8.69 us
    all_to_all x2 -> x1, waiting for transfers between devices: 95.1 us -> 51.8 us  [exchange(): lax.all_to_all(values, GROUP, split_axis=0, concat_axis=0, tiled=True)]
    dot_general x9 -> x0, matrix products: 37.8 us -> none  [the longest x2 7.82 us: gated_side(): jnp.einsum('kic,ch->hki', normed, w_second, preferred_element_type=jnp.fl...]
    all_to_all x1 -> x2, blocking collectives: 111 us -> 148 us  [exchange(): lax.all_to_all(values, GROUP, split_axis=0, concat_axis=0, tiled=True)]
    pallas_call x0 -> x4, Pallas kernels: none -> 28.9 us  [the longest x1 11.6 us: make_finish(): pl.pallas_call(finish_kernel, grid=(columns // LANES,), in_specs=[pl.Bloc...]
    unnamed x28 -> x23, local copies, waits for them, and re-layouts: 29.8 us -> 6.75 us
    unnamed x1 -> x0, other arithmetic: 14.1 us -> none
    reduce_sum x4 -> x0, other arithmetic: 10.5 us -> none  [the longest x2 7.69 us: layer_norm(): second = jnp.mean(center * center, axis=axis_index, keepdims=True)]
    all_to_all x2 -> x1, starting transfers between devices: 17.3 us -> 8.69 us  [exchange(): lax.all_to_all(values, GROUP, split_axis=0, concat_axis=0, tiled=True)]
  transfers between devices with their start and end apart: 2 -> 1, of which waited for: 2 -> 1; matrix products, arithmetic and copies ran while one was open for 3% -> 0% of each run, Pallas kernels for 0% -> 0%
where the time goes in v1:
time: 247 us; the launch traced here: 246 us
  blocking collectives  148 us (60%)
  waiting for transfers between devices  51.8 us (21%)
  Pallas kernels  28.9 us (12%)
  starting transfers between devices  8.69 us (4%)
  local copies, waits for them, and re-layouts  7.66 us (3%)
    all_to_all x2, blocking collectives, exchange(): lax.all_to_all(values, GROUP, split_axis=0, concat_axis=0, tiled=True)  148 us
    all_to_all x1, waiting for transfers between devices, exchange(): lax.all_to_all(values, GROUP, split_axis=0, concat_axis=0, tiled=True)  51.8 us
    pallas_call x1, Pallas kernels, make_finish(): pl.pallas_call(finish_kernel, grid=(columns // LANES,), in_specs=[pl.Bloc...  11.6 us
    pallas_call x1, Pallas kernels, make_sides(): pl.pallas_call(sides_kernel, grid=(steps,), in_specs=[pl.BlockSpec(memory...  9.03 us
    all_to_all x1, starting transfers between devices, exchange(): lax.all_to_all(values, GROUP, split_axis=0, concat_axis=0, tiled=True)  8.69 us
    unnamed x23, local copies, waits for them, and re-layouts  6.75 us
    pallas_call x1, Pallas kernels, make_product(): pl.pallas_call(product_kernel, grid=(columns // block,), in_specs=[pl.Blo...  6.1 us
  transfers between devices with their start and end apart: 1, of which 1 were waited for; matrix products, arithmetic and copies ran while one was open for 0% of the time, Pallas kernels for 0%

profile of v1, /device:TPU:1, one launch (start us, length us, event | category | flops | bytes accessed | tf_op | source)
XLA Modules:
  0.0 245.9 jit_solution(7561252562745690699)
XLA Ops:
  0.6 0.8 dynamic_slice.3.own_ref
  1.4 1.6 copy-done
  3.0 0.0 copy-start.2
  3.0 0.8 copy-done.2
  3.8 0.8 copy-done.3
  4.5 0.8 copy-done.4
  5.3 0.8 copy-done.5
  6.0 0.7 copy-done.8
  6.7 9.0 %sides.1 = (bf16[8,1024,128]{2,1,0:T(8,128)(2,1)S(1)}, bf16[128,2,8,1024]{3,2,1,0:T(8,128)(2,1)}) custom-call(s32[8]{0:T(128)S(1)} %dynamic_slice.3.own_ref, s32[8,1,128]{2,1,0:T(1,128)S(1)} %bitcast.5, bf16[8,1024,128]{2,1,0:T(8,128)(2,1)S(1)} %copy-done, bf16[128,128]{1,0:T(8,128)(2,1)S(1)} %copy-done.2, bf16[128,128]{1,0:T(8,128)(2,1)S(1)} %copy-done.3, ...), custom_call_target="tpu_custom_call" | custom-call | tf_op jit(solution)/shard_map/sides/pallas_call | solution.py:44
  15.7 110.7 %all_to_all.15.left_ref.right_ref = bf16[128,2,8,1024]{3,2,1,0:T(8,128)(2,1)} all-to-all(bf16[128,2,8,1024]{3,2,1,0:T(8,128)(2,1)} %get-tuple-element.7), channel_id=1, replica_groups=mesh['dp'=2,'row'=32,'chan'=4] {'row','chan'}, dimensions={0} | all-to-all | bytes 8388608 | tf_op jit(solution)/shard_map/all_to_all | solution.py:189
  126.4 0.0 copy-done.1
  126.4 6.1 %product.1 = bf16[128,8,1024]{2,1,0:T(8,128)(2,1)} custom-call(bf16[128,2,8,1024]{3,2,1,0:T(8,128)(2,1)} %all_to_all.15.left_ref.right_ref, bf16[128,2,8,1024]{3,2,1,0:T(8,128)(2,1)} %all_to_all.15.left_ref.right_ref), custom_call_target="tpu_custom_call" | custom-call | tf_op jit(solution)/shard_map/product/pallas_call | solution.py:81
  132.5 8.7 %all-to-all-start.1 = ((bf16[128,8,1024]{2,1,0:T(8,128)(2,1)}), bf16[128,8,1024]{2,1,0:T(8,128)(2,1)S(1)}, u32[]{:S(2)}, u32[]{:S(2)}) async-start(bf16[128,8,1024]{2,1,0:T(8,128)(2,1)} %product.1), calls=%async_computation.1 | async-start | bytes 4194304 | tf_op jit(solution)/shard_map/all_to_all | solution.py:189
  141.2 0.0 copy-done.10
  141.2 0.1 copy.14.wd_ref
  141.4 0.1 copy.13
  141.5 0.1 broadcast_select_fusion
  141.6 51.8 %all-to-all-done.1.x_ref = bf16[128,8,1024]{2,1,0:T(8,128)(2,1)S(1)} async-done(((bf16[128,8,1024]{2,1,0:T(8,128)(2,1)}), bf16[128,8,1024]{2,1,0:T(8,128)(2,1)S(1)}, u32[]{:S(2)}, u32[]{:S(2)}) %all-to-all-start.1) | async-done | bytes 2097184 | tf_op jit(solution)/shard_map/all_to_all | solution.py:189
  193.4 1.3 copy-done.9
  194.8 0.0 copy-done.6
  194.8 0.0 copy-done.7
  194.8 11.6 %finish.1 = (bf16[8,1024,128]{2,1,0:T(8,128)(2,1)}, f32[64,8,1024]{2,1,0:T(8,128)S(1)}, bf16[128,8,512]{2,1,0:T(8,128)(2,1)S(1)}) custom-call(bf16[128,8,1024]{2,1,0:T(8,128)(2,1)} %copy-done.9, bf16[8,1024,128]{2,1,0:T(8,128)(2,1)} %base_ref.1, bf16[8,1024,128]{2,1,0:T(8,128)(2,1)} %copy-done.1, bf16[128,128]{1,0:T(8,128)(2,1)S(1)} %copy-done.6, ...), custom_call_target="tpu_custom_call" | custom-call | tf_op jit(solution)/shard_map/finish/pallas_call | solution.py:133
  206.3 37.3 %all_to_all.16.mirror_ref = bf16[128,8,512]{2,1,0:T(8,128)(2,1)S(1)} all-to-all(bf16[128,8,512]{2,1,0:T(8,128)(2,1)S(1)} %get-tuple-element.11), channel_id=1, replica_groups=mesh['dp'=2,'row'=32,'chan'=4] {'row','chan'}, dimensions={0} | all-to-all | bytes 2097152 | tf_op jit(solution)/shard_map/all_to_all | solution.py:189
  243.7 2.2 add.21
  (13 shorter events, 0.1 us)
Async XLA Ops:
  1.4 1.6 copy-start
  3.0 0.8 copy-start.2
  3.7 0.8 copy-start.3
  4.5 0.8 copy-start.4
  5.3 0.8 copy-start.5
  6.0 0.7 copy-start.8
  15.7 110.7 %copy-start.1 = (bf16[8,1024,128]{2,1,0:T(8,128)(2,1)}, bf16[8,1024,128]{2,1,0:T(8,128)(2,1)S(1)}, u32[]{:S(2)}) copy-start(bf16[8,1024,128]{2,1,0:T(8,128)(2,1)S(1)} %get-tuple-element.8.normed_ref) | copy-start | bytes 6291460
  132.5 8.7 %copy-start.10 = (bf16[128,64]{0,1:T(8,128)(2,1)S(1)}, bf16[128,64]{0,1:T(8,128)(2,1)}, u32[]{:S(2)}) copy-start(bf16[128,64]{0,1:T(8,128)(2,1)} %param.17) | copy-start | bytes 49156
  132.5 62.3 %copy-start.6 = (bf16[128,128]{1,0:T(8,128)(2,1)S(1)}, bf16[128,128]{1,0:T(8,128)(2,1)}, u32[]{:S(2)}) copy-start(bf16[128,128]{1,0:T(8,128)(2,1)} %wg_ref.1) | copy-start | bytes 98308
  132.5 62.3 %copy-start.7 = (bf16[128,128]{1,0:T(8,128)(2,1)S(1)}, bf16[128,128]{1,0:T(8,128)(2,1)}, u32[]{:S(2)}) copy-start(bf16[128,128]{1,0:T(8,128)(2,1)} %wo_ref.1) | copy-start | bytes 98308
  132.5 60.9 %all-to-all-start.1 = ((bf16[128,8,1024]{2,1,0:T(8,128)(2,1)}), bf16[128,8,1024]{2,1,0:T(8,128)(2,1)S(1)}, u32[]{:S(2)}, u32[]{:S(2)}) async-start(bf16[128,8,1024]{2,1,0:T(8,128)(2,1)} %product.1), calls=%async_computation.1 | async-start | bytes 4194304 | tf_op jit(solution)/shard_map/all_to_all | solution.py:189
  193.4 1.3 copy-start.9

commit v2 on v0

v2 whole, which is shorter than its diff:
```python
import jax
import jax.numpy as jnp
from jax import lax
from jax.experimental import pallas as pl
from jax.experimental.pallas import tpu as pltpu
from jax.sharding import PartitionSpec as P

EPS = 1e-05
GROUP = ("row", "chan")
ROWS = 8
LANES = 128
VMEM_LIMIT = 24 * 1024 * 1024
SIDES_AT_ONCE = 4
FINISH_AT_ONCE = 4
ADD_AT_ONCE = 2

F32 = jnp.float32
BF16 = jnp.bfloat16
NT = (((1,), (1,)), ((), ()))
TN = (((0,), (0,)), ((), ()))


def params():
    return pltpu.CompilerParams(vmem_limit_bytes=VMEM_LIMIT)


def whole(memory_space=pltpu.VMEM):
    return pl.BlockSpec(memory_space=memory_space)


def in_hbm(*values):
    return [pltpu.with_memory_space_constraint(value, pltpu.HBM) for value in values]


def lanes(step):
    return pl.ds(pl.multiple_of(step * LANES, LANES), LANES)


def sides_kernel(
    mask_hbm, flat_hbm, x_hbm, wag_hbm, wap_hbm, wbg_hbm, wbp_hbm,
    normed_ref, sides_ref,
    mask_ref, flat_ref, x_ref, w_ref, scratch, sems, few_sems,
):
    rows, columns, channels = x_ref.shape
    steps = columns // LANES
    few = [pltpu.make_async_copy(mask_hbm, mask_ref, few_sems.at[0])]
    few.append(pltpu.make_async_copy(flat_hbm, flat_ref, few_sems.at[1]))
    for n, w in enumerate((wag_hbm, wap_hbm, wbg_hbm, wbp_hbm)):
        few.append(pltpu.make_async_copy(w, w_ref.at[n], few_sems.at[2 + n]))

    def block(step):
        return pltpu.make_async_copy(x_hbm.at[:, lanes(step)], x_ref.at[:, lanes(step)], sems.at[step])

    block(0).start()
    for copy in few:
        copy.start()
    for step in range(1, steps):
        block(step).start()
    for copy in few:
        copy.wait()
    first = lax.axis_index(GROUP) * rows

    def one(step, slot):
        x = x_ref[:, lanes(step)].astype(F32).reshape(rows * LANES, channels)
        center = x - jnp.mean(x, axis=1, keepdims=True)
        second = jnp.mean(center * center, axis=1, keepdims=True)
        normed = (center * lax.rsqrt(second + EPS)).astype(BF16)
        normed_ref[:, lanes(step)] = normed.reshape(rows, LANES, channels)
        mask = mask_ref[step].astype(F32)
        w = jnp.concatenate([w_ref[n] for n in range(4)], axis=1)
        out = lax.dot_general(w, normed, (((0,), (1,)), ((), ())), preferred_element_type=F32)
        for side in range(2):
            gate = out[2 * side * LANES : (2 * side + 1) * LANES]
            proj = out[(2 * side + 1) * LANES : (2 * side + 2) * LANES]
            both = jax.nn.sigmoid(gate) * proj
            for k in range(rows):
                keep = mask * flat_ref[first + k].astype(F32)
                scratch[slot, side, pl.ds(k, LANES, stride=rows), :] = both[:, k * LANES : (k + 1) * LANES] * keep
            sides_ref[:, side, :, lanes(step)] = scratch[slot, side].reshape(LANES, rows, LANES).astype(BF16)

    def body(turn, carry):
        for slot in range(SIDES_AT_ONCE):
            block(turn * SIDES_AT_ONCE + slot).wait()
        for slot in range(SIDES_AT_ONCE):
            one(turn * SIDES_AT_ONCE + slot, slot)
        return carry

    lax.fori_loop(0, steps // SIDES_AT_ONCE, body, 0)


def make_sides(pair_rep, token_mask, w_a_gate, w_a_proj, w_b_gate, w_b_proj):
    rows, columns, channels = pair_rep.shape
    steps = columns // LANES
    return pl.pallas_call(
        sides_kernel,
        in_specs=[whole(pltpu.HBM)] * 7,
        out_specs=[whole(), whole()],
        out_shape=[
            jax.ShapeDtypeStruct(pair_rep.shape, BF16),
            jax.ShapeDtypeStruct((LANES, 2, rows, columns), BF16),
        ],
        scratch_shapes=[
            pltpu.VMEM((steps, 1, LANES), jnp.int32),
            pltpu.SMEM(token_mask.shape, jnp.int32),
            pltpu.VMEM(pair_rep.shape, BF16),
            pltpu.VMEM((4, channels, LANES), BF16),
            pltpu.VMEM((SIDES_AT_ONCE, 2, rows * LANES, LANES), F32),
            pltpu.SemaphoreType.DMA((steps,)),
            pltpu.SemaphoreType.DMA((6,)),
        ],
        compiler_params=params(),
        name="sides",
    )(
        *in_hbm(
            token_mask.reshape(steps, 1, LANES), token_mask, pair_rep, w_a_gate, w_a_proj, w_b_gate, w_b_proj
        )
    )


def product_kernel(sides_ref, out_ref):
    sources, _, rows, columns = sides_ref.shape
    depth = sources * rows
    block = 256

    def body(step, carry):
        here = pl.ds(pl.multiple_of(step * block, block), block)
        left = sides_ref[:, 0, :, here].reshape(depth, block)
        right = sides_ref[:, 1].reshape(depth, columns)
        prod = lax.dot_general(left, right, TN, preferred_element_type=F32)
        owners = block // rows
        out_ref[pl.ds(step * owners, owners)] = prod.reshape(owners, rows, columns).astype(BF16)
        return carry

    lax.fori_loop(0, columns // block, body, 0)


def make_product(sides):
    sources, _, rows, columns = sides.shape
    return pl.pallas_call(
        product_kernel,
        in_specs=[whole()],
        out_specs=whole(),
        out_shape=jax.ShapeDtypeStruct((columns // rows, rows, columns), BF16),
        compiler_params=params(),
        name="product",
    )(sides)


def finish_kernel(
    x_ref, base_ref, normed_ref, wg_ref, wo_ref, wd_ref,
    upd_hbm, own_ref, mirror_ref,
    upd_ref, scratch, wide, sems,
):
    rows, columns, channels = base_ref.shape
    owners = LANES // rows
    bins = wd_ref.shape[0]
    steps = columns // LANES

    def send(step):
        return pltpu.make_async_copy(upd_ref.at[:, lanes(step)], upd_hbm.at[:, lanes(step)], sems.at[step])

    def one(step, scratch_ref, wide_ref):
        here = lanes(step)
        x = x_ref[:, :, here].astype(F32)
        center = x - jnp.mean(x, axis=0, keepdims=True)
        second = jnp.mean(center * center, axis=0, keepdims=True)
        scratch_ref[...] = (center * lax.rsqrt(second + EPS)).reshape(scratch_ref.shape)
        tri = jnp.concatenate(
            [scratch_ref[pl.ds(r, LANES, stride=rows), :].astype(BF16) for r in range(rows)], axis=1
        )
        projected = lax.dot_general(tri, wo_ref[...], TN, preferred_element_type=F32)
        normed = normed_ref[:, here].reshape(rows * LANES, channels)
        gate = jax.nn.sigmoid(jnp.dot(normed, wg_ref[...], preferred_element_type=F32))
        base = base_ref[:, here].reshape(rows * LANES, channels).astype(F32)
        updated = (base + gate * projected).astype(BF16)
        upd_ref[:, here] = updated.reshape(rows, LANES, channels)
        wide_ref[...] = updated.astype(F32)
        weight = wd_ref[...]
        own = lax.dot_general(weight, updated, NT, preferred_element_type=F32)
        for r in range(rows):
            own_ref[r, :, here] = own[:, r * LANES : (r + 1) * LANES]
        zero = jnp.zeros_like(weight)
        twice = jnp.concatenate(
            [jnp.concatenate([weight, zero], axis=1), jnp.concatenate([zero, weight], axis=1)], axis=0
        )
        for pair in range(rows // 2):
            picks = []
            for s in (2 * pair, 2 * pair + 1):
                parts = [wide_ref[pl.ds(d * rows + s, rows, stride=LANES), :] for d in range(owners)]
                picks.append(jnp.concatenate(parts, axis=0).astype(BF16))
            mirror = lax.dot_general(jnp.concatenate(picks, axis=1), twice, NT, preferred_element_type=F32)
            mirror_ref[pl.ds(step * owners, owners), :, pair * 2 * bins : (pair + 1) * 2 * bins] = mirror.reshape(
                owners, rows, 2 * bins
            ).astype(BF16)

    def body(turn, carry):
        for slot in range(FINISH_AT_ONCE):
            one(turn * FINISH_AT_ONCE + slot, scratch.at[slot], wide.at[slot])
        for slot in range(FINISH_AT_ONCE):
            send(turn * FINISH_AT_ONCE + slot).start()
        return carry

    lax.fori_loop(0, steps // FINISH_AT_ONCE, body, 0)
    for step in range(steps):
        send(step).wait()


def make_finish(product, pair_rep, normed, w_gate, w_out, w_dist):
    rows, columns, channels = pair_rep.shape
    bins = w_dist.shape[1]
    return pl.pallas_call(
        finish_kernel,
        in_specs=[whole()] * 6,
        out_specs=[whole(pltpu.HBM), whole(), whole()],
        out_shape=[
            jax.ShapeDtypeStruct(pair_rep.shape, BF16),
            jax.ShapeDtypeStruct((rows, bins, columns), F32),
            jax.ShapeDtypeStruct((columns // rows, rows, rows * bins), BF16),
        ],
        scratch_shapes=[
            pltpu.VMEM(pair_rep.shape, BF16),
            pltpu.VMEM((FINISH_AT_ONCE, LANES * rows, LANES), F32),
            pltpu.VMEM((FINISH_AT_ONCE, rows * LANES, channels), F32),
            pltpu.SemaphoreType.DMA((columns // LANES,)),
        ],
        compiler_params=params(),
        name="finish",
    )(product, pair_rep, normed, w_gate, w_out, w_dist.T)


def add_kernel(own_ref, mirror_ref, out_hbm, out_ref, sems):
    rows, bins, columns = own_ref.shape
    owners = LANES // rows
    steps = columns // LANES

    def send(step):
        return pltpu.make_async_copy(out_ref.at[step], out_hbm.at[:, :, lanes(step)], sems.at[step])

    def one(step):
        mirror = mirror_ref[pl.ds(step * owners, owners)].reshape(LANES, rows * bins)
        turned = mirror.astype(F32).T
        flat_ref = out_ref.at[step].reshape(bins * rows, LANES)
        for r in range(rows):
            total = own_ref[r, :, lanes(step)] + turned[r * bins : (r + 1) * bins]
            flat_ref[pl.ds(r, bins, stride=rows), :] = total

    def body(turn, carry):
        for slot in range(ADD_AT_ONCE):
            one(turn * ADD_AT_ONCE + slot)
        for slot in range(ADD_AT_ONCE):
            send(turn * ADD_AT_ONCE + slot).start()
        return carry

    lax.fori_loop(0, steps // ADD_AT_ONCE, body, 0)
    for step in range(steps):
        send(step).wait()


def make_add(own, mirror):
    rows, bins, columns = own.shape
    steps = columns // LANES
    return pl.pallas_call(
        add_kernel,
        in_specs=[whole(), whole()],
        out_specs=whole(pltpu.HBM),
        out_shape=jax.ShapeDtypeStruct((bins, rows, columns), F32),
        scratch_shapes=[
            pltpu.VMEM((steps, bins, rows, LANES), F32),
            pltpu.SemaphoreType.DMA((steps,)),
        ],
        compiler_params=params(),
        name="add",
    )(own, mirror)


def exchange(values):
    return lax.all_to_all(values, GROUP, split_axis=0, concat_axis=0, tiled=True)


def local(pair_rep, token_mask, w_a_gate, w_a_proj, w_b_gate, w_b_proj, w_gate, w_out, w_dist):
    normed, sides = make_sides(pair_rep, token_mask, w_a_gate, w_a_proj, w_b_gate, w_b_proj)
    product = make_product(exchange(sides))
    updated, own, mirror = make_finish(exchange(product), pair_rep, normed, w_gate, w_out, w_dist)
    return (updated, make_add(own, exchange(mirror)))


def solution(mesh):
    in_specs = (P(("dp", "row", "chan"), None, None), P("dp"), P(), P(), P(), P(), P(), P(), P())
    out_specs = (P(("dp", "row", "chan"), None, None), P(None, ("dp", "row", "chan"), None))
    return jax.shard_map(local, mesh=mesh, in_specs=in_specs, out_specs=out_specs, check_vma=False)
```

time: 350 us -> 229 us (0.65)
  blocking collectives: 111 us -> 208 us
  waiting for transfers between devices: 95.1 us -> 0 us
  local copies, waits for them, and re-layouts: 51.6 us -> 0.03 us
  matrix products: 37.8 us -> 0 us
  other arithmetic: 34.3 us -> 0 us
  Pallas kernels: 0 us -> 19.8 us
  starting transfers between devices: 17.3 us -> 0 us
    all_to_all x1 -> x3, blocking collectives: 111 us -> 208 us  [exchange(): lax.all_to_all(values, GROUP, split_axis=0, concat_axis=0, tiled=True)]
    all_to_all x2 -> x0, waiting for transfers between devices: 95.1 us -> none  [the longest x1 48.4 us: local(): lax.all_to_all(mirror_split(updated, devices), ('row', 'chan'), split_axi...]
    dot_general x9 -> x0, matrix products: 37.8 us -> none  [the longest x2 7.82 us: gated_side(): jnp.einsum('kic,ch->hki', normed, w_second, preferred_element_type=jnp.fl...]
    unnamed x28 -> x8, local copies, waits for them, and re-layouts: 29.8 us -> 0.03 us
    pallas_call x0 -> x4, Pallas kernels: none -> 19.8 us  [the longest x1 7.99 us: make_finish(): pl.pallas_call(finish_kernel, in_specs=[whole()] * 6, out_specs=[whole(pl...]
    all_to_all x2 -> x0, starting transfers between devices: 17.3 us -> none  [the longest x1 9.63 us: to_row_layout(): lax.all_to_all(stacked, ('row', 'chan'), split_axis=2, concat_axis=1, til...]
    unnamed x1 -> x0, other arithmetic: 14.1 us -> none
    reduce_sum x4 -> x0, other arithmetic: 10.5 us -> none  [the longest x2 7.69 us: layer_norm(): second = jnp.mean(center * center, axis=axis_index, keepdims=True)]
  transfers between devices with their start and end apart: 2 -> 0, of which waited for: 2 -> 0; matrix products, arithmetic and copies ran while one was open for 3% -> 0% of each run, Pallas kernels for 0% -> 0%
where the time goes in v2:
time: 229 us
  blocking collectives  208 us (91%)
  Pallas kernels  19.8 us (9%)
    all_to_all x3, blocking collectives, exchange(): lax.all_to_all(values, GROUP, split_axis=0, concat_axis=0, tiled=True)  208 us
    pallas_call x1, Pallas kernels, make_finish(): pl.pallas_call(finish_kernel, in_specs=[whole()] * 6, out_specs=[whole(pl...  7.99 us
    pallas_call x1, Pallas kernels, make_sides(): pl.pallas_call(sides_kernel, in_specs=[whole(pltpu.HBM)] * 7, out_specs=[...  7.28 us

profile of v2, /device:TPU:1, one launch (start us, length us, event | category | flops | bytes accessed | tf_op | source)
XLA Modules:
  0.0 228.5 jit_solution(15430906982829843368)
XLA Ops:
  0.6 7.3 %sides.1 = (bf16[8,1024,128]{2,1,0:T(8,128)(2,1)S(1)}, bf16[128,2,8,1024]{3,2,1,0:T(8,128)(2,1)S(1)}) custom-call(s32[8,1,128]{2,1,0:T(1,128)} %bitcast.3, s32[1024]{0:T(1024)} %flat_hbm.1, bf16[8,1024,128]{2,1,0:T(8,128)(2,1)} %base_ref.1, bf16[128,128]{1,0:T(8,128)(2,1)} %wag_hbm.1, bf16[128,128]{1,0:T(8,128)(2,1)} %wap_hbm.1, bf16[128,128]{1,0:T(8,128)(2,1)} %wbg_hbm.1, ...), custom_call_target="tpu_custom_call" | custom-call | tf_op jit(solution)/shard_map/sides/pallas_call | solution.py:94
  7.9 110.3 %all_to_all.15.sides_ref = bf16[128,2,8,1024]{3,2,1,0:T(8,128)(2,1)S(1)} all-to-all(bf16[128,2,8,1024]{3,2,1,0:T(8,128)(2,1)S(1)} %get-tuple-element.7), channel_id=1, replica_groups=mesh['dp'=2,'row'=32,'chan'=4] {'row','chan'}, dimensions={0} | all-to-all | bytes 8388608 | tf_op jit(solution)/shard_map/all_to_all | solution.py:277
  118.3 3.0 %product.1 = bf16[128,8,1024]{2,1,0:T(8,128)(2,1)S(1)} custom-call(bf16[128,2,8,1024]{3,2,1,0:T(8,128)(2,1)S(1)} %all_to_all.15.sides_ref), custom_call_target="tpu_custom_call" | custom-call | tf_op jit(solution)/shard_map/product/pallas_call | solution.py:139
  121.3 0.0 copy-start
  121.3 0.0 copy-start.1
  121.3 0.0 copy-start.2
  121.3 0.0 copy-start.3
  121.4 60.2 %all_to_all.16.x_ref = bf16[128,8,1024]{2,1,0:T(8,128)(2,1)S(1)} all-to-all(bf16[128,8,1024]{2,1,0:T(8,128)(2,1)S(1)} %product.1), channel_id=1, replica_groups=mesh['dp'=2,'row'=32,'chan'=4] {'row','chan'}, dimensions={0} | all-to-all | bytes 4194304 | tf_op jit(solution)/shard_map/all_to_all | solution.py:277
  181.6 0.0 copy-done
  181.6 0.0 copy-done.1
  181.6 0.0 copy-done.2
  181.6 0.0 copy-done.3
  181.6 8.0 %finish.1 = (bf16[8,1024,128]{2,1,0:T(8,128)(2,1)}, f32[8,64,1024]{2,1,0:T(8,128)S(1)}, bf16[128,8,512]{2,1,0:T(8,128)(2,1)S(1)}) custom-call(bf16[128,8,1024]{2,1,0:T(8,128)(2,1)S(1)} %all_to_all.16.x_ref, bf16[8,1024,128]{2,1,0:T(8,128)(2,1)S(1)} %copy-done, bf16[8,1024,128]{2,1,0:T(8,128)(2,1)S(1)} %get-tuple-element.8.normed_ref, ...), custom_call_target="tpu_custom_call" | custom-call | tf_op jit(solution)/shard_map/finish/pallas_call | solution.py:211
  189.6 37.3 %all_to_all.17.mirror_ref = bf16[128,8,512]{2,1,0:T(8,128)(2,1)S(1)} all-to-all(bf16[128,8,512]{2,1,0:T(8,128)(2,1)S(1)} %get-tuple-element.11), channel_id=1, replica_groups=mesh['dp'=2,'row'=32,'chan'=4] {'row','chan'}, dimensions={0} | all-to-all | bytes 2097152 | tf_op jit(solution)/shard_map/all_to_all | solution.py:277
  227.0 1.5 add.1
Async XLA Ops:
  121.3 60.3 %copy-start = (bf16[8,1024,128]{2,1,0:T(8,128)(2,1)S(1)}, bf16[8,1024,128]{2,1,0:T(8,128)(2,1)}, u32[]{:S(2)}) copy-start(bf16[8,1024,128]{2,1,0:T(8,128)(2,1)} %base_ref.1) | copy-start | bytes 6291460
  121.3 60.3 %copy-start.1 = (bf16[128,128]{1,0:T(8,128)(2,1)S(1)}, bf16[128,128]{1,0:T(8,128)(2,1)}, u32[]{:S(2)}) copy-start(bf16[128,128]{1,0:T(8,128)(2,1)} %wg_ref.1) | copy-start | bytes 98308
  121.3 60.3 %copy-start.2 = (bf16[128,128]{1,0:T(8,128)(2,1)S(1)}, bf16[128,128]{1,0:T(8,128)(2,1)}, u32[]{:S(2)}) copy-start(bf16[128,128]{1,0:T(8,128)(2,1)} %wo_ref.1) | copy-start | bytes 98308
  121.3 60.3 %copy-start.3 = (bf16[128,64]{0,1:T(8,128)(2,1)S(1)}, bf16[128,64]{0,1:T(8,128)(2,1)}, u32[]{:S(2)}) copy-start(bf16[128,64]{0,1:T(8,128)(2,1)} %param.17) | copy-start | bytes 49156

commit v3 on v2

--- a/solution.py
+++ b/solution.py
@@ -6,7 +6,9 @@
 from jax.sharding import PartitionSpec as P
 
 EPS = 1e-05
-GROUP = ("row", "chan")
+PLACES = ("ylo", "z", "core", "chan")
+GROUP = ("z", "chan", "core", "ylo")
+GRID = (8, 4, 2, 2)
 ROWS = 8
 LANES = 128
 VMEM_LIMIT = 24 * 1024 * 1024
@@ -58,7 +60,7 @@
         block(step).start()
     for copy in few:
         copy.wait()
-    first = lax.axis_index(GROUP) * rows
+    first = lax.axis_index(PLACES) * rows
 
     def one(step, slot):
         x = x_ref[:, lanes(step)].astype(F32).reshape(rows * LANES, channels)
@@ -117,18 +119,28 @@
     )
 
 
+def by_place(block, owners):
+    across = GRID[1] * GRID[2]
+    runs = GRID[0] * across // owners
+    return lax.rem(block, runs) * (owners // across), block // runs
+
+
 def product_kernel(sides_ref, out_ref):
     sources, _, rows, columns = sides_ref.shape
     depth = sources * rows
     block = 256
+    owners = block // rows
+    deep = owners // (GRID[1] * GRID[2])
 
     def body(step, carry):
         here = pl.ds(pl.multiple_of(step * block, block), block)
         left = sides_ref[:, 0, :, here].reshape(depth, block)
         right = sides_ref[:, 1].reshape(depth, columns)
         prod = lax.dot_general(left, right, TN, preferred_element_type=F32)
-        owners = block // rows
-        out_ref[pl.ds(step * owners, owners)] = prod.reshape(owners, rows, columns).astype(BF16)
+        prod = prod.reshape(deep, GRID[2], GRID[1], rows, columns).astype(BF16)
+        z, ylo = by_place(step, owners)
+        for core in range(GRID[2]):
+            out_ref[pl.ds(z, deep), :, core, ylo] = prod[:, core]
         return carry
 
     lax.fori_loop(0, columns // block, body, 0)
@@ -136,30 +148,32 @@
 
 def make_product(sides):
     sources, _, rows, columns = sides.shape
-    return pl.pallas_call(
+    product = pl.pallas_call(
         product_kernel,
         in_specs=[whole()],
         out_specs=whole(),
-        out_shape=jax.ShapeDtypeStruct((columns // rows, rows, columns), BF16),
+        out_shape=jax.ShapeDtypeStruct(GRID + (rows, columns), BF16),
         compiler_params=params(),
         name="product",
     )(sides)
+    return product.reshape(columns // rows, rows, columns)
 
 
 def finish_kernel(
     x_ref, base_ref, normed_ref, wg_ref, wo_ref, wd_ref,
     upd_hbm, own_ref, mirror_ref,
-    upd_ref, scratch, wide, sems,
+    upd_ref, scratch, wide, stage, sems,
 ):
     rows, columns, channels = base_ref.shape
     owners = LANES // rows
     bins = wd_ref.shape[0]
     steps = columns // LANES
+    deep = owners // (GRID[1] * GRID[2])
 
     def send(step):
         return pltpu.make_async_copy(upd_ref.at[:, lanes(step)], upd_hbm.at[:, lanes(step)], sems.at[step])
 
-    def one(step, scratch_ref, wide_ref):
+    def one(step, scratch_ref, wide_ref, stage_ref):
         here = lanes(step)
         x = x_ref[:, :, here].astype(F32)
         center = x - jnp.mean(x, axis=0, keepdims=True)
@@ -183,19 +197,19 @@
         twice = jnp.concatenate(
             [jnp.concatenate([weight, zero], axis=1), jnp.concatenate([zero, weight], axis=1)], axis=0
         )
+        z, ylo = by_place(step, owners)
         for pair in range(rows // 2):
-            picks = []
-            for s in (2 * pair, 2 * pair + 1):
-                parts = [wide_ref[pl.ds(d * rows + s, rows, stride=LANES), :] for d in range(owners)]
-                picks.append(jnp.concatenate(parts, axis=0).astype(BF16))
+            picks = [wide_ref[pl.ds(2 * pair + s, LANES, stride=rows), :].astype(BF16) for s in range(2)]
             mirror = lax.dot_general(jnp.concatenate(picks, axis=1), twice, NT, preferred_element_type=F32)
-            mirror_ref[pl.ds(step * owners, owners), :, pair * 2 * bins : (pair + 1) * 2 * bins] = mirror.reshape(
-                owners, rows, 2 * bins
-            ).astype(BF16)
+            for r in range(rows):
+                stage_ref[pair, pl.ds(r, owners, stride=rows), :] = mirror[r * owners : (r + 1) * owners]
+            turned = stage_ref[pair].reshape(deep, GRID[2], GRID[1], rows, 2 * bins).astype(BF16)
+            for core in range(GRID[2]):
+                mirror_ref[pl.ds(z, deep), :, core, ylo, :, pair * 2 * bins : (pair + 1) * 2 * bins] = turned[:, core]
 
     def body(turn, carry):
         for slot in range(FINISH_AT_ONCE):
-            one(turn * FINISH_AT_ONCE + slot, scratch.at[slot], wide.at[slot])
+            one(turn * FINISH_AT_ONCE + slot, scratch.at[slot], wide.at[slot], stage.at[slot])
         for slot in range(FINISH_AT_ONCE):
             send(turn * FINISH_AT_ONCE + slot).start()
         return carry
@@ -215,12 +229,13 @@
         out_shape=[
             jax.ShapeDtypeStruct(pair_rep.shape, BF16),
             jax.ShapeDtypeStruct((rows, bins, columns), F32),
-            jax.ShapeDtypeStruct((columns // rows, rows, rows * bins), BF16),
+            jax.ShapeDtypeStruct(GRID + (rows, rows * bins), BF16),
         ],
         scratch_shapes=[
             pltpu.VMEM(pair_rep.shape, BF16),
             pltpu.VMEM((FINISH_AT_ONCE, LANES * rows, LANES), F32),
             pltpu.VMEM((FINISH_AT_ONCE, rows * LANES, channels), F32),
+            pltpu.VMEM((FINISH_AT_ONCE, rows // 2, LANES, LANES), F32),
             pltpu.SemaphoreType.DMA((columns // LANES,)),
         ],
         compiler_params=params(),
@@ -232,13 +247,15 @@
     rows, bins, columns = own_ref.shape
     owners = LANES // rows
     steps = columns // LANES
+    deep = owners // (GRID[1] * GRID[2])
 
     def send(step):
         return pltpu.make_async_copy(out_ref.at[step], out_hbm.at[:, :, lanes(step)], sems.at[step])
 
     def one(step):
-        mirror = mirror_ref[pl.ds(step * owners, owners)].reshape(LANES, rows * bins)
-        turned = mirror.astype(F32).T
+        z, ylo = by_place(step, owners)
+        cores = [mirror_ref[pl.ds(z, deep), :, core, ylo] for core in range(GRID[2])]
+        turned = jnp.stack(cores, axis=1).reshape(LANES, rows * bins).astype(F32).T
         flat_ref = out_ref.at[step].reshape(bins * rows, LANES)
         for r in range(rows):
             total = own_ref[r, :, lanes(step)] + turned[r * bins : (r + 1) * bins]
@@ -281,10 +298,14 @@
     normed, sides = make_sides(pair_rep, token_mask, w_a_gate, w_a_proj, w_b_gate, w_b_proj)
     product = make_product(exchange(sides))
     updated, own, mirror = make_finish(exchange(product), pair_rep, normed, w_gate, w_out, w_dist)
-    return (updated, make_add(own, exchange(mirror)))
+    arrived = exchange(mirror.reshape((-1,) + mirror.shape[4:])).reshape(mirror.shape)
+    return (updated, make_add(own, arrived))
 
 
 def solution(mesh):
-    in_specs = (P(("dp", "row", "chan"), None, None), P("dp"), P(), P(), P(), P(), P(), P(), P())
-    out_specs = (P(("dp", "row", "chan"), None, None), P(None, ("dp", "row", "chan"), None))
-    return jax.shard_map(local, mesh=mesh, in_specs=in_specs, out_specs=out_specs, check_vma=False)
+    z, chan, core, ylo = GRID
+    split = jax.sharding.Mesh(mesh.devices.reshape(-1, ylo, z, core, chan), ("dp",) + PLACES)
+    rows = ("dp",) + PLACES
+    in_specs = (P(rows, None, None), P("dp"), P(), P(), P(), P(), P(), P(), P())
+    out_specs = (P(rows, None, None), P(None, rows, None))
+    return jax.shard_map(local, mesh=split, in_specs=in_specs, out_specs=out_specs, check_vma=False)

time: 229 us -> 224 us (0.978)
  blocking collectives: 208 us -> 205 us
    all_to_all x3, blocking collectives: 208 us -> 205 us  [exchange(): lax.all_to_all(values, GROUP, split_axis=0, concat_axis=0, tiled=True)]
where the time goes in v3:
time: 224 us
  blocking collectives  205 us (92%)
  Pallas kernels  18.3 us (8%)
    all_to_all x3, blocking collectives, exchange(): lax.all_to_all(values, GROUP, split_axis=0, concat_axis=0, tiled=True)  205 us
    pallas_call x1, Pallas kernels, make_sides(): pl.pallas_call(sides_kernel, in_specs=[whole(pltpu.HBM)] * 7, out_specs=[...  7.28 us
    pallas_call x1, Pallas kernels, make_finish(): pl.pallas_call(finish_kernel, in_specs=[whole()] * 6, out_specs=[whole(pl...  6.44 us

profile of v3, /device:TPU:1, one launch (start us, length us, event | category | flops | bytes accessed | tf_op | source)
XLA Modules:
  0.0 224.0 jit_solution(8667191992614037253)
XLA Ops:
  0.6 7.3 %sides.1 = (bf16[8,1024,128]{2,1,0:T(8,128)(2,1)S(1)}, bf16[128,2,8,1024]{3,2,1,0:T(8,128)(2,1)S(1)}) custom-call(s32[8,1,128]{2,1,0:T(1,128)} %bitcast.9, s32[1024]{0:T(1024)} %flat_hbm.1, bf16[8,1024,128]{2,1,0:T(8,128)(2,1)} %base_ref.1, bf16[128,128]{1,0:T(8,128)(2,1)} %wag_hbm.1, bf16[128,128]{1,0:T(8,128)(2,1)} %wap_hbm.1, bf16[128,128]{1,0:T(8,128)(2,1)} %wbg_hbm.1, ...), custom_call_target="tpu_custom_call" | custom-call | tf_op jit(solution)/shard_map/sides/pallas_call | solution.py:96
  7.9 111.3 %all_to_all.15.sides_ref = bf16[128,2,8,1024]{3,2,1,0:T(8,128)(2,1)S(1)} all-to-all(bf16[128,2,8,1024]{3,2,1,0:T(8,128)(2,1)S(1)} %get-tuple-element.7), channel_id=1, replica_groups=mesh['dp'=2,'ylo'=2,'z'=8,'core'=2,'chan'=4] {'z','chan','core','ylo'}, dimensions={0} | all-to-all | bytes 8388608 | tf_op jit(solution)/shard_map/all_to_all | solution.py:294
  119.2 3.0 %product.1 = bf16[8,4,2,2,8,1024]{5,4,3,2,1,0:T(8,128)(2,1)S(1)} custom-call(bf16[128,2,8,1024]{3,2,1,0:T(8,128)(2,1)S(1)} %all_to_all.15.sides_ref), custom_call_target="tpu_custom_call" | custom-call | tf_op jit(solution)/shard_map/product/pallas_call | solution.py:151
  122.3 0.0 copy-start
  122.3 0.0 copy-start.1
  122.3 0.0 copy-start.2
  122.3 0.0 copy-start.3
  122.3 57.6 %all_to_all.16.x_ref = bf16[128,8,1024]{2,1,0:T(8,128)(2,1)S(1)} all-to-all(bf16[128,8,1024]{2,1,0:T(8,128)(2,1)S(1)} %bitcast.5), channel_id=1, replica_groups=mesh['dp'=2,'ylo'=2,'z'=8,'core'=2,'chan'=4] {'z','chan','core','ylo'}, dimensions={0} | all-to-all | bytes 4194304 | tf_op jit(solution)/shard_map/all_to_all | solution.py:294
  179.9 0.0 copy-done
  179.9 0.0 copy-done.1
  179.9 0.0 copy-done.2
  179.9 0.0 copy-done.3
  179.9 6.4 %finish.1 = (bf16[8,1024,128]{2,1,0:T(8,128)(2,1)}, f32[8,64,1024]{2,1,0:T(8,128)S(1)}, bf16[8,4,2,2,8,512]{5,4,3,2,1,0:T(8,128)(2,1)S(1)}) custom-call(bf16[128,8,1024]{2,1,0:T(8,128)(2,1)S(1)} %all_to_all.16.x_ref, bf16[8,1024,128]{2,1,0:T(8,128)(2,1)S(1)} %copy-done, bf16[8,1024,128]{2,1,0:T(8,128)(2,1)S(1)} %get-tuple-element.8.normed_ref, ...), custom_call_target="tpu_custom_call" | custom-call | tf_op jit(solution)/shard_map/finish/pallas_call | solution.py:225
  186.4 36.0 %all_to_all.17 = bf16[128,8,512]{2,1,0:T(8,128)(2,1)S(1)} all-to-all(bf16[128,8,512]{2,1,0:T(8,128)(2,1)S(1)} %bitcast.7), channel_id=1, replica_groups=mesh['dp'=2,'ylo'=2,'z'=8,'core'=2,'chan'=4] {'z','chan','core','ylo'}, dimensions={0} | all-to-all | bytes 2097152 | tf_op jit(solution)/shard_map/all_to_all | solution.py:294
  222.4 1.5 add.1
Async XLA Ops:
  122.3 57.6 %copy-start = (bf16[8,1024,128]{2,1,0:T(8,128)(2,1)S(1)}, bf16[8,1024,128]{2,1,0:T(8,128)(2,1)}, u32[]{:S(2)}) copy-start(bf16[8,1024,128]{2,1,0:T(8,128)(2,1)} %base_ref.1) | copy-start | bytes 6291460
  122.3 57.6 %copy-start.1 = (bf16[128,128]{1,0:T(8,128)(2,1)S(1)}, bf16[128,128]{1,0:T(8,128)(2,1)}, u32[]{:S(2)}) copy-start(bf16[128,128]{1,0:T(8,128)(2,1)} %wg_ref.1) | copy-start | bytes 98308
  122.3 57.6 %copy-start.2 = (bf16[128,128]{1,0:T(8,128)(2,1)S(1)}, bf16[128,128]{1,0:T(8,128)(2,1)}, u32[]{:S(2)}) copy-start(bf16[128,128]{1,0:T(8,128)(2,1)} %wo_ref.1) | copy-start | bytes 98308
  122.3 57.6 %copy-start.3 = (bf16[128,64]{0,1:T(8,128)(2,1)S(1)}, bf16[128,64]{0,1:T(8,128)(2,1)}, u32[]{:S(2)}) copy-start(bf16[128,64]{0,1:T(8,128)(2,1)} %param.17) | copy-start | bytes 49156

commit v4 on v3

--- a/solution.py
+++ b/solution.py
@@ -13,8 +13,8 @@
 LANES = 128
 VMEM_LIMIT = 24 * 1024 * 1024
 SIDES_AT_ONCE = 4
-FINISH_AT_ONCE = 4
-ADD_AT_ONCE = 2
+FINISH_AT_ONCE = 2
+ADD_AT_ONCE = 1
 
 F32 = jnp.float32
 BF16 = jnp.bfloat16
@@ -143,7 +143,7 @@
             out_ref[pl.ds(z, deep), :, core, ylo] = prod[:, core]
         return carry
 
-    lax.fori_loop(0, columns // block, body, 0)
+    lax.fori_loop(0, columns // block, body, 0, unroll=True)
 
 
 def make_product(sides):
@@ -176,11 +176,16 @@
     def one(step, scratch_ref, wide_ref, stage_ref):
         here = lanes(step)
         x = x_ref[:, :, here].astype(F32)
-        center = x - jnp.mean(x, axis=0, keepdims=True)
-        second = jnp.mean(center * center, axis=0, keepdims=True)
-        scratch_ref[...] = (center * lax.rsqrt(second + EPS)).reshape(scratch_ref.shape)
+        mean = jnp.mean(x, axis=0, keepdims=True)
+        center = x - mean
+        scale = lax.rsqrt(jnp.mean(center * center, axis=0, keepdims=True) + EPS)
+        scratch_ref[...] = x.reshape(scratch_ref.shape)
         tri = jnp.concatenate(
-            [scratch_ref[pl.ds(r, LANES, stride=rows), :].astype(BF16) for r in range(rows)], axis=1
+            [
+                ((scratch_ref[pl.ds(r, LANES, stride=rows), :] - mean[0, r : r + 1]) * scale[0, r : r + 1]).astype(BF16)
+                for r in range(rows)
+            ],
+            axis=1,
         )
         projected = lax.dot_general(tri, wo_ref[...], TN, preferred_element_type=F32)
         normed = normed_ref[:, here].reshape(rows * LANES, channels)
@@ -214,7 +219,7 @@
             send(turn * FINISH_AT_ONCE + slot).start()
         return carry
 
-    lax.fori_loop(0, steps // FINISH_AT_ONCE, body, 0)
+    lax.fori_loop(0, steps // FINISH_AT_ONCE, body, 0, unroll=True)
     for step in range(steps):
         send(step).wait()
 
@@ -268,7 +273,7 @@
             send(turn * ADD_AT_ONCE + slot).start()
         return carry
 
-    lax.fori_loop(0, steps // ADD_AT_ONCE, body, 0)
+    lax.fori_loop(0, steps // ADD_AT_ONCE, body, 0, unroll=True)
     for step in range(steps):
         send(step).wait()
 

time: 224 us -> 223 us (level)
  no operation moved by 1% of the time
where the time goes in v4:
time: 223 us; the launch traced here: 222 us
  blocking collectives  205 us (92%)
  Pallas kernels  16.5 us (7%)
    all_to_all x3, blocking collectives, exchange(): lax.all_to_all(values, GROUP, split_axis=0, concat_axis=0, tiled=True)  205 us
    pallas_call x1, Pallas kernels, make_sides(): pl.pallas_call(sides_kernel, in_specs=[whole(pltpu.HBM)] * 7, out_specs=[...  7.26 us
    pallas_call x1, Pallas kernels, make_finish(): pl.pallas_call(finish_kernel, in_specs=[whole()] * 6, out_specs=[whole(pl...  5.4 us

profile of v4, /device:TPU:1, one launch (start us, length us, event | category | flops | bytes accessed | tf_op | source)
XLA Modules:
  0.0 222.3 jit_solution(2574504642611452974)
XLA Ops:
  0.6 7.3 %sides.1 = (bf16[8,1024,128]{2,1,0:T(8,128)(2,1)S(1)}, bf16[128,2,8,1024]{3,2,1,0:T(8,128)(2,1)S(1)}) custom-call(s32[8,1,128]{2,1,0:T(1,128)} %bitcast.9, s32[1024]{0:T(1024)} %flat_hbm.1, bf16[8,1024,128]{2,1,0:T(8,128)(2,1)} %base_ref.1, bf16[128,128]{1,0:T(8,128)(2,1)} %wag_hbm.1, bf16[128,128]{1,0:T(8,128)(2,1)} %wap_hbm.1, bf16[128,128]{1,0:T(8,128)(2,1)} %wbg_hbm.1, ...), custom_call_target="tpu_custom_call" | custom-call | tf_op jit(solution)/shard_map/sides/pallas_call | solution.py:96
  7.9 111.3 %all_to_all.15.sides_ref = bf16[128,2,8,1024]{3,2,1,0:T(8,128)(2,1)S(1)} all-to-all(bf16[128,2,8,1024]{3,2,1,0:T(8,128)(2,1)S(1)} %get-tuple-element.7), channel_id=1, replica_groups=mesh['dp'=2,'ylo'=2,'z'=8,'core'=2,'chan'=4] {'z','chan','core','ylo'}, dimensions={0} | all-to-all | bytes 8388608 | tf_op jit(solution)/shard_map/all_to_all | solution.py:299
  119.2 2.4 %product.1 = bf16[8,4,2,2,8,1024]{5,4,3,2,1,0:T(8,128)(2,1)S(1)} custom-call(bf16[128,2,8,1024]{3,2,1,0:T(8,128)(2,1)S(1)} %all_to_all.15.sides_ref), custom_call_target="tpu_custom_call" | custom-call | tf_op jit(solution)/shard_map/product/pallas_call | solution.py:151
  121.6 0.0 copy-start
  121.6 0.0 copy-start.1
  121.6 0.0 copy-start.2
  121.6 0.0 copy-start.3
  121.6 57.6 %all_to_all.16.x_ref = bf16[128,8,1024]{2,1,0:T(8,128)(2,1)S(1)} all-to-all(bf16[128,8,1024]{2,1,0:T(8,128)(2,1)S(1)} %bitcast.5), channel_id=1, replica_groups=mesh['dp'=2,'ylo'=2,'z'=8,'core'=2,'chan'=4] {'z','chan','core','ylo'}, dimensions={0} | all-to-all | bytes 4194304 | tf_op jit(solution)/shard_map/all_to_all | solution.py:299
  179.2 0.0 copy-done
  179.2 0.0 copy-done.1
  179.2 0.0 copy-done.2
  179.2 0.0 copy-done.3
  179.2 5.4 %finish.1 = (bf16[8,1024,128]{2,1,0:T(8,128)(2,1)}, f32[8,64,1024]{2,1,0:T(8,128)S(1)}, bf16[8,4,2,2,8,512]{5,4,3,2,1,0:T(8,128)(2,1)S(1)}) custom-call(bf16[128,8,1024]{2,1,0:T(8,128)(2,1)S(1)} %all_to_all.16.x_ref, bf16[8,1024,128]{2,1,0:T(8,128)(2,1)S(1)} %copy-done, bf16[8,1024,128]{2,1,0:T(8,128)(2,1)S(1)} %get-tuple-element.8.normed_ref, ...), custom_call_target="tpu_custom_call" | custom-call | tf_op jit(solution)/shard_map/finish/pallas_call | solution.py:230
  184.6 36.0 %all_to_all.17 = bf16[128,8,512]{2,1,0:T(8,128)(2,1)S(1)} all-to-all(bf16[128,8,512]{2,1,0:T(8,128)(2,1)S(1)} %bitcast.7), channel_id=1, replica_groups=mesh['dp'=2,'ylo'=2,'z'=8,'core'=2,'chan'=4] {'z','chan','core','ylo'}, dimensions={0} | all-to-all | bytes 2097152 | tf_op jit(solution)/shard_map/all_to_all | solution.py:299
  220.7 1.5 add.1
Async XLA Ops:
  121.6 57.6 %copy-start = (bf16[8,1024,128]{2,1,0:T(8,128)(2,1)S(1)}, bf16[8,1024,128]{2,1,0:T(8,128)(2,1)}, u32[]{:S(2)}) copy-start(bf16[8,1024,128]{2,1,0:T(8,128)(2,1)} %base_ref.1) | copy-start | bytes 6291460
  121.6 57.6 %copy-start.1 = (bf16[128,128]{1,0:T(8,128)(2,1)S(1)}, bf16[128,128]{1,0:T(8,128)(2,1)}, u32[]{:S(2)}) copy-start(bf16[128,128]{1,0:T(8,128)(2,1)} %wg_ref.1) | copy-start | bytes 98308
  121.6 57.6 %copy-start.2 = (bf16[128,128]{1,0:T(8,128)(2,1)S(1)}, bf16[128,128]{1,0:T(8,128)(2,1)}, u32[]{:S(2)}) copy-start(bf16[128,128]{1,0:T(8,128)(2,1)} %wo_ref.1) | copy-start | bytes 98308
  121.6 57.6 %copy-start.3 = (bf16[128,64]{0,1:T(8,128)(2,1)S(1)}, bf16[128,64]{0,1:T(8,128)(2,1)}, u32[]{:S(2)}) copy-start(bf16[128,64]{0,1:T(8,128)(2,1)} %param.17) | copy-start | bytes 49156

commit v5 on v4

--- a/solution.py
+++ b/solution.py
@@ -12,7 +12,7 @@
 ROWS = 8
 LANES = 128
 VMEM_LIMIT = 24 * 1024 * 1024
-SIDES_AT_ONCE = 4
+SIDES_AT_ONCE = (2, 6)
 FINISH_AT_ONCE = 2
 ADD_AT_ONCE = 1
 
@@ -80,14 +80,13 @@
                 scratch[slot, side, pl.ds(k, LANES, stride=rows), :] = both[:, k * LANES : (k + 1) * LANES] * keep
             sides_ref[:, side, :, lanes(step)] = scratch[slot, side].reshape(LANES, rows, LANES).astype(BF16)
 
-    def body(turn, carry):
-        for slot in range(SIDES_AT_ONCE):
-            block(turn * SIDES_AT_ONCE + slot).wait()
-        for slot in range(SIDES_AT_ONCE):
-            one(turn * SIDES_AT_ONCE + slot, slot)
-        return carry
-
-    lax.fori_loop(0, steps // SIDES_AT_ONCE, body, 0)
+    at = 0
+    for size in SIDES_AT_ONCE:
+        for slot in range(size):
+            block(at + slot).wait()
+        for slot in range(size):
+            one(at + slot, slot)
+        at += size
 
 
 def make_sides(pair_rep, token_mask, w_a_gate, w_a_proj, w_b_gate, w_b_proj):
@@ -106,7 +105,7 @@
             pltpu.SMEM(token_mask.shape, jnp.int32),
             pltpu.VMEM(pair_rep.shape, BF16),
             pltpu.VMEM((4, channels, LANES), BF16),
-            pltpu.VMEM((SIDES_AT_ONCE, 2, rows * LANES, LANES), F32),
+            pltpu.VMEM((max(SIDES_AT_ONCE), 2, rows * LANES, LANES), F32),
             pltpu.SemaphoreType.DMA((steps,)),
             pltpu.SemaphoreType.DMA((6,)),
         ],

time: 223 us -> 222 us (level)
  no operation moved by 1% of the time
where the time goes in v5:
time: 222 us
  blocking collectives  205 us (92%)
  Pallas kernels  16.4 us (7%)
    all_to_all x3, blocking collectives, exchange(): lax.all_to_all(values, GROUP, split_axis=0, concat_axis=0, tiled=True)  205 us
    pallas_call x1, Pallas kernels, make_sides(): pl.pallas_call(sides_kernel, in_specs=[whole(pltpu.HBM)] * 7, out_specs=[...  7.17 us
    pallas_call x1, Pallas kernels, make_finish(): pl.pallas_call(finish_kernel, in_specs=[whole()] * 6, out_specs=[whole(pl...  5.4 us

profile of v5, /device:TPU:1, one launch (start us, length us, event | category | flops | bytes accessed | tf_op | source)
XLA Modules:
  0.0 222.2 jit_solution(14269243366045894101)
XLA Ops:
  0.6 7.2 %sides.1 = (bf16[8,1024,128]{2,1,0:T(8,128)(2,1)S(1)}, bf16[128,2,8,1024]{3,2,1,0:T(8,128)(2,1)S(1)}) custom-call(s32[8,1,128]{2,1,0:T(1,128)} %bitcast.9, s32[1024]{0:T(1024)} %flat_hbm.1, bf16[8,1024,128]{2,1,0:T(8,128)(2,1)} %base_ref.1, bf16[128,128]{1,0:T(8,128)(2,1)} %wag_hbm.1, bf16[128,128]{1,0:T(8,128)(2,1)} %wap_hbm.1, bf16[128,128]{1,0:T(8,128)(2,1)} %wbg_hbm.1, ...), custom_call_target="tpu_custom_call" | custom-call | tf_op jit(solution)/shard_map/sides/pallas_call | solution.py:95
  7.8 111.3 %all_to_all.15.sides_ref = bf16[128,2,8,1024]{3,2,1,0:T(8,128)(2,1)S(1)} all-to-all(bf16[128,2,8,1024]{3,2,1,0:T(8,128)(2,1)S(1)} %get-tuple-element.7), channel_id=1, replica_groups=mesh['dp'=2,'ylo'=2,'z'=8,'core'=2,'chan'=4] {'z','chan','core','ylo'}, dimensions={0} | all-to-all | bytes 8388608 | tf_op jit(solution)/shard_map/all_to_all | solution.py:298
  119.1 2.4 %product.1 = bf16[8,4,2,2,8,1024]{5,4,3,2,1,0:T(8,128)(2,1)S(1)} custom-call(bf16[128,2,8,1024]{3,2,1,0:T(8,128)(2,1)S(1)} %all_to_all.15.sides_ref), custom_call_target="tpu_custom_call" | custom-call | tf_op jit(solution)/shard_map/product/pallas_call | solution.py:150
  121.5 0.0 copy-start
  121.5 0.0 copy-start.1
  121.5 0.0 copy-start.2
  121.5 0.0 copy-start.3
  121.5 57.6 %all_to_all.16.x_ref = bf16[128,8,1024]{2,1,0:T(8,128)(2,1)S(1)} all-to-all(bf16[128,8,1024]{2,1,0:T(8,128)(2,1)S(1)} %bitcast.5), channel_id=1, replica_groups=mesh['dp'=2,'ylo'=2,'z'=8,'core'=2,'chan'=4] {'z','chan','core','ylo'}, dimensions={0} | all-to-all | bytes 4194304 | tf_op jit(solution)/shard_map/all_to_all | solution.py:298
  179.1 0.0 copy-done
  179.1 0.0 copy-done.1
  179.1 0.0 copy-done.2
  179.1 0.0 copy-done.3
  179.1 5.4 %finish.1 = (bf16[8,1024,128]{2,1,0:T(8,128)(2,1)}, f32[8,64,1024]{2,1,0:T(8,128)S(1)}, bf16[8,4,2,2,8,512]{5,4,3,2,1,0:T(8,128)(2,1)S(1)}) custom-call(bf16[128,8,1024]{2,1,0:T(8,128)(2,1)S(1)} %all_to_all.16.x_ref, bf16[8,1024,128]{2,1,0:T(8,128)(2,1)S(1)} %copy-done, bf16[8,1024,128]{2,1,0:T(8,128)(2,1)S(1)} %get-tuple-element.8.normed_ref, ...), custom_call_target="tpu_custom_call" | custom-call | tf_op jit(solution)/shard_map/finish/pallas_call | solution.py:229
  184.5 36.0 %all_to_all.17 = bf16[128,8,512]{2,1,0:T(8,128)(2,1)S(1)} all-to-all(bf16[128,8,512]{2,1,0:T(8,128)(2,1)S(1)} %bitcast.7), channel_id=1, replica_groups=mesh['dp'=2,'ylo'=2,'z'=8,'core'=2,'chan'=4] {'z','chan','core','ylo'}, dimensions={0} | all-to-all | bytes 2097152 | tf_op jit(solution)/shard_map/all_to_all | solution.py:298
  220.6 1.5 add.1
Async XLA Ops:
  121.5 57.6 %copy-start = (bf16[8,1024,128]{2,1,0:T(8,128)(2,1)S(1)}, bf16[8,1024,128]{2,1,0:T(8,128)(2,1)}, u32[]{:S(2)}) copy-start(bf16[8,1024,128]{2,1,0:T(8,128)(2,1)} %base_ref.1) | copy-start | bytes 6291460
  121.5 57.6 %copy-start.1 = (bf16[128,128]{1,0:T(8,128)(2,1)S(1)}, bf16[128,128]{1,0:T(8,128)(2,1)}, u32[]{:S(2)}) copy-start(bf16[128,128]{1,0:T(8,128)(2,1)} %wg_ref.1) | copy-start | bytes 98308
  121.5 57.6 %copy-start.2 = (bf16[128,128]{1,0:T(8,128)(2,1)S(1)}, bf16[128,128]{1,0:T(8,128)(2,1)}, u32[]{:S(2)}) copy-start(bf16[128,128]{1,0:T(8,128)(2,1)} %wo_ref.1) | copy-start | bytes 98308
  121.5 57.6 %copy-start.3 = (bf16[128,64]{0,1:T(8,128)(2,1)S(1)}, bf16[128,64]{0,1:T(8,128)(2,1)}, u32[]{:S(2)}) copy-start(bf16[128,64]{0,1:T(8,128)(2,1)} %param.17) | copy-start | bytes 49156

commit v6 on v5

--- a/solution.py
+++ b/solution.py
@@ -65,7 +65,8 @@
     def one(step, slot):
         x = x_ref[:, lanes(step)].astype(F32).reshape(rows * LANES, channels)
         center = x - jnp.mean(x, axis=1, keepdims=True)
-        second = jnp.mean(center * center, axis=1, keepdims=True)
+        share = jnp.full((channels, LANES), 1 / channels, BF16)
+        second = jnp.dot((center * center).astype(BF16), share, preferred_element_type=F32)
         normed = (center * lax.rsqrt(second + EPS)).astype(BF16)
         normed_ref[:, lanes(step)] = normed.reshape(rows, LANES, channels)
         mask = mask_ref[step].astype(F32)

time: 222 us -> 222 us (level)
  no operation moved by 1% of the time
where the time goes in v6:
time: 222 us
  blocking collectives  205 us (92%)
  Pallas kernels  16.2 us (7%)
    all_to_all x3, blocking collectives, exchange(): lax.all_to_all(values, GROUP, split_axis=0, concat_axis=0, tiled=True)  205 us
    pallas_call x1, Pallas kernels, make_sides(): pl.pallas_call(sides_kernel, in_specs=[whole(pltpu.HBM)] * 7, out_specs=[...  6.92 us
    pallas_call x1, Pallas kernels, make_finish(): pl.pallas_call(finish_kernel, in_specs=[whole()] * 6, out_specs=[whole(pl...  5.4 us

profile of v6, /device:TPU:1, one launch (start us, length us, event | category | flops | bytes accessed | tf_op | source)
XLA Modules:
  0.0 222.0 jit_solution(2785779624843214461)
XLA Ops:
  0.6 6.9 %sides.1 = (bf16[8,1024,128]{2,1,0:T(8,128)(2,1)S(1)}, bf16[128,2,8,1024]{3,2,1,0:T(8,128)(2,1)S(1)}) custom-call(s32[8,1,128]{2,1,0:T(1,128)} %bitcast.9, s32[1024]{0:T(1024)} %flat_hbm.1, bf16[8,1024,128]{2,1,0:T(8,128)(2,1)} %base_ref.1, bf16[128,128]{1,0:T(8,128)(2,1)} %wag_hbm.1, bf16[128,128]{1,0:T(8,128)(2,1)} %wap_hbm.1, bf16[128,128]{1,0:T(8,128)(2,1)} %wbg_hbm.1, ...), custom_call_target="tpu_custom_call" | custom-call | tf_op jit(solution)/shard_map/sides/pallas_call | solution.py:96
  7.6 111.3 %all_to_all.15.sides_ref = bf16[128,2,8,1024]{3,2,1,0:T(8,128)(2,1)S(1)} all-to-all(bf16[128,2,8,1024]{3,2,1,0:T(8,128)(2,1)S(1)} %get-tuple-element.7), channel_id=1, replica_groups=mesh['dp'=2,'ylo'=2,'z'=8,'core'=2,'chan'=4] {'z','chan','core','ylo'}, dimensions={0} | all-to-all | bytes 8388608 | tf_op jit(solution)/shard_map/all_to_all | solution.py:299
  118.9 2.4 %product.1 = bf16[8,4,2,2,8,1024]{5,4,3,2,1,0:T(8,128)(2,1)S(1)} custom-call(bf16[128,2,8,1024]{3,2,1,0:T(8,128)(2,1)S(1)} %all_to_all.15.sides_ref), custom_call_target="tpu_custom_call" | custom-call | tf_op jit(solution)/shard_map/product/pallas_call | solution.py:151
  121.2 0.0 copy-start
  121.3 0.0 copy-start.1
  121.3 0.0 copy-start.2
  121.3 0.0 copy-start.3
  121.3 57.6 %all_to_all.16.x_ref = bf16[128,8,1024]{2,1,0:T(8,128)(2,1)S(1)} all-to-all(bf16[128,8,1024]{2,1,0:T(8,128)(2,1)S(1)} %bitcast.5), channel_id=1, replica_groups=mesh['dp'=2,'ylo'=2,'z'=8,'core'=2,'chan'=4] {'z','chan','core','ylo'}, dimensions={0} | all-to-all | bytes 4194304 | tf_op jit(solution)/shard_map/all_to_all | solution.py:299
  178.9 0.0 copy-done
  178.9 0.0 copy-done.1
  178.9 0.0 copy-done.2
  178.9 0.0 copy-done.3
  178.9 5.4 %finish.1 = (bf16[8,1024,128]{2,1,0:T(8,128)(2,1)}, f32[8,64,1024]{2,1,0:T(8,128)S(1)}, bf16[8,4,2,2,8,512]{5,4,3,2,1,0:T(8,128)(2,1)S(1)}) custom-call(bf16[128,8,1024]{2,1,0:T(8,128)(2,1)S(1)} %all_to_all.16.x_ref, bf16[8,1024,128]{2,1,0:T(8,128)(2,1)S(1)} %copy-done, bf16[8,1024,128]{2,1,0:T(8,128)(2,1)S(1)} %get-tuple-element.8.normed_ref, ...), custom_call_target="tpu_custom_call" | custom-call | tf_op jit(solution)/shard_map/finish/pallas_call | solution.py:230
  184.3 36.0 %all_to_all.17 = bf16[128,8,512]{2,1,0:T(8,128)(2,1)S(1)} all-to-all(bf16[128,8,512]{2,1,0:T(8,128)(2,1)S(1)} %bitcast.7), channel_id=1, replica_groups=mesh['dp'=2,'ylo'=2,'z'=8,'core'=2,'chan'=4] {'z','chan','core','ylo'}, dimensions={0} | all-to-all | bytes 2097152 | tf_op jit(solution)/shard_map/all_to_all | solution.py:299
  220.4 1.5 add.1
Async XLA Ops:
  121.2 57.6 %copy-start = (bf16[8,1024,128]{2,1,0:T(8,128)(2,1)S(1)}, bf16[8,1024,128]{2,1,0:T(8,128)(2,1)}, u32[]{:S(2)}) copy-start(bf16[8,1024,128]{2,1,0:T(8,128)(2,1)} %base_ref.1) | copy-start | bytes 6291460
  121.3 57.6 %copy-start.1 = (bf16[128,128]{1,0:T(8,128)(2,1)S(1)}, bf16[128,128]{1,0:T(8,128)(2,1)}, u32[]{:S(2)}) copy-start(bf16[128,128]{1,0:T(8,128)(2,1)} %wg_ref.1) | copy-start | bytes 98308
  121.3 57.6 %copy-start.2 = (bf16[128,128]{1,0:T(8,128)(2,1)S(1)}, bf16[128,128]{1,0:T(8,128)(2,1)}, u32[]{:S(2)}) copy-start(bf16[128,128]{1,0:T(8,128)(2,1)} %wo_ref.1) | copy-start | bytes 98308
  121.3 57.6 %copy-start.3 = (bf16[128,64]{0,1:T(8,128)(2,1)S(1)}, bf16[128,64]{0,1:T(8,128)(2,1)}, u32[]{:S(2)}) copy-start(bf16[128,64]{0,1:T(8,128)(2,1)} %param.17) | copy-start | bytes 49156
